TPU v7x, 32 devices: a whole 2x2x4 slice. The times are simulated.
32 devices in a mesh: replica: 2 (over x), shard: 16 (over z, y, core).
Axes of the slice: x: 2, y: 2, z: 4, core: 2. Of those that a mesh axis runs over, the one named last changes fastest.
Arguments:
- tokens: bfloat16 [8192, 2048], P(('replica', 'shard')), may hold values from -6 to 6
- segments: int32 [32, 256], P(('replica', 'shard')), may hold values from 0 to 3, never falling along the last dimension, each value on 1 to 128 neighbouring positions
- attend_weight: bfloat16 [2048, 6144], P('shard'), may hold values from -0.125 to 0.125
- attend_bias: bfloat16 [6144], P('shard'), may hold values from -3 to 3
- output_weight: bfloat16 [2048, 2048], P('shard'), may hold values from -0.75 to 0.75
- attend_gain: bfloat16 [2048], P('shard'), may hold values from 0.5 to 1.5
- attend_shift: bfloat16 [2048], P('shard'), may hold values from -1 to 1
- expand_weight: bfloat16 [2048, 11264], P('shard'), may hold values from -0.125 to 0.125
- shrink_weight: bfloat16 [2048, 5632], P('shard'), may hold values from -0.15625 to 0.15625
- dense_gain: bfloat16 [2048], P('shard'), may hold values from 0.5 to 1.5
- dense_shift: bfloat16 [2048], P('shard'), may hold values from -1 to 1
- cotangent: bfloat16 [8192, 2048], P(('replica', 'shard')), may hold values from -6 to 6
Outputs:
- layer_output: bfloat16 [8192, 2048], P(('replica', 'shard'))
- tokens_gradient: bfloat16 [8192, 2048], P(('replica', 'shard'))
- attend_weight_gradient: float32 [2048, 6144], P('shard')
- attend_bias_gradient: float32 [6144], P('shard')
- output_weight_gradient: float32 [2048, 2048], P('shard')
- attend_gain_gradient: float32 [2048], P('shard')
- attend_shift_gradient: float32 [2048], P('shard')
- expand_weight_gradient: float32 [2048, 11264], P('shard')
- shrink_weight_gradient: float32 [2048, 5632], P('shard')
- dense_gain_gradient: float32 [2048], P('shard')
- dense_shift_gradient: float32 [2048], P('shard')
Inputs may be any that keep to these rules, and one draw needn't show every extreme that they name: `segments`: along each sequence the segment numbers never fall, and a segment holds at most 128 tokens.
All inputs are finite; a program needn't handle non-finite values.
Results may differ from a plain program's by a relative error of at most 0.015.
Values may be sent and summed in bfloat16 or wider, within the bound.
No kernel may reach another device: no remote copies, remote signals or barrier semaphores. Data moves between devices by JAX's collectives and lax.ppermute only.
A program may use at most 640 MiB of HBM per device.

v0:
```python
import math

import jax
import jax.numpy as jnp
from jax import lax
from jax.sharding import PartitionSpec as P

D = 2048
HEADS = 32
HEAD_DIM = 64
FF = 5632
ROT = 16


EPSILON = 1e-05


def norm_parts(values):
    center = jnp.mean(values, axis=-1, keepdims=True)
    centered = values - center
    variance = jnp.mean(centered * centered, axis=-1, keepdims=True)
    inverse = lax.rsqrt(variance + EPSILON)
    return (centered * inverse, inverse)


def norm_backward(slope, normed, inverse, gain_row):
    scaled = slope * gain_row
    first_mean = jnp.mean(scaled, axis=-1, keepdims=True)
    second_mean = jnp.mean(scaled * normed, axis=-1, keepdims=True)
    return inverse * (scaled - first_mean - normed * second_mean)


def rotary_tables(segment_row):
    length = segment_row.shape[0]
    places = jnp.arange(length)
    same_doc = segment_row[:, None] == segment_row[None, :]
    earlier = places[:, None] > places[None, :]
    position = jnp.sum(jnp.where(same_doc & earlier, 1.0, 0.0), axis=1).astype(jnp.float32)
    frequency = jnp.exp(jnp.arange(ROT // 2).astype(jnp.float32) * (-2.0 * math.log(10000.0) / ROT))
    angles = position[:, None] * frequency[None, :]
    allowed = same_doc & (places[:, None] >= places[None, :])
    return (jnp.cos(angles), jnp.sin(angles), allowed)


def rotate(values, cosines, sine_table):
    half_rot = ROT // 2
    first_half = values[..., :half_rot]
    second_half = values[..., half_rot:ROT]
    cos_wide = cosines[:, None, :]
    sin_wide = sine_table[:, None, :]
    return jnp.concatenate(
        [
            first_half * cos_wide - second_half * sin_wide,
            second_half * cos_wide + first_half * sin_wide,
            values[..., ROT:],
        ],
        axis=-1,
    )


def unrotate(slope, cosines, sine_table):
    half_rot = ROT // 2
    first_half = slope[..., :half_rot]
    second_half = slope[..., half_rot:ROT]
    cos_wide = cosines[:, None, :]
    sin_wide = sine_table[:, None, :]
    return jnp.concatenate(
        [
            first_half * cos_wide + second_half * sin_wide,
            second_half * cos_wide - first_half * sin_wide,
            slope[..., ROT:],
        ],
        axis=-1,
    )


def rows_product(left_side, right_side):
    return jnp.dot(left_side, right_side, preferred_element_type=jnp.float32)


def last_product(left_side, right_side):
    return lax.dot_general(
        left_side, right_side, (((1,), (1,)), ((), ())), preferred_element_type=jnp.float32
    )


def first_product(left_side, right_side):
    return lax.dot_general(
        left_side, right_side, (((0,), (0,)), ((), ())), preferred_element_type=jnp.float32
    )


def score_block(queries, keys_all, allowed):
    scaled = jnp.einsum(
        "thd,shd->hts", queries, keys_all, preferred_element_type=jnp.float32
    ) * HEAD_DIM ** (-0.5)
    return jnp.where(allowed[None], scaled, -1e30)


def fold_rows(left_side, shard_rows):
    return rows_product(left_side, shard_rows)


def shards(
    tokens,
    segments,
    attend_weight,
    attend_bias,
    output_weight,
    attend_gain,
    attend_shift,
    expand_weight,
    shrink_weight,
    dense_gain,
    dense_shift,
    cotangent,
):
    token_count = tokens.shape[0]
    gathered = (
        lax.all_gather(attend_bias, "shard", axis=0, tiled=True),
        lax.all_gather(attend_gain, "shard", axis=0, tiled=True),
        lax.all_gather(attend_shift, "shard", axis=0, tiled=True),
        lax.all_gather(dense_gain, "shard", axis=0, tiled=True),
        lax.all_gather(dense_shift, "shard", axis=0, tiled=True),
    )
    bias_full = gathered[0].astype(jnp.float32)
    gain_one = gathered[1].astype(jnp.float32)
    shift_one = gathered[2].astype(jnp.float32)
    gain_two = gathered[3].astype(jnp.float32)
    shift_two = gathered[4].astype(jnp.float32)
    start_rows = tokens.astype(jnp.float32)
    normed_one, inverse_one = norm_parts(start_rows)
    attend_input = (normed_one * gain_one + shift_one).astype(jnp.bfloat16)
    joined = (
        fold_rows(attend_input, lax.all_gather(attend_weight, "shard", axis=0, tiled=True))
        + bias_full
    )
    cosines, sine_table, allowed = rotary_tables(segments[0])
    shaped = joined.reshape(token_count, 3, HEADS, HEAD_DIM)
    queries = rotate(shaped[:, 0], cosines, sine_table).astype(jnp.bfloat16)
    keys_all = rotate(shaped[:, 1], cosines, sine_table).astype(jnp.bfloat16)
    values_all = shaped[:, 2].astype(jnp.bfloat16)
    scores = score_block(queries, keys_all, allowed)
    highest = jnp.max(scores, axis=-1, keepdims=True)
    shifted = jnp.exp(scores - highest)
    denominator = jnp.sum(shifted, axis=-1, keepdims=True)
    log_norm = highest + jnp.log(denominator)
    weights = (shifted / denominator).astype(jnp.bfloat16)
    attended = (
        jnp.einsum("hts,shd->thd", weights, values_all, preferred_element_type=jnp.float32)
        .reshape(token_count, D)
        .astype(jnp.bfloat16)
    )
    middle = start_rows + last_product(
        attended, lax.all_gather(output_weight, "shard", axis=0, tiled=True)
    )
    normed_two, inverse_two = norm_parts(middle)
    dense_input = (normed_two * gain_two + shift_two).astype(jnp.bfloat16)
    gate_up = fold_rows(dense_input, lax.all_gather(expand_weight, "shard", axis=0, tiled=True))
    gate_part = gate_up[:, :FF]
    up_part = gate_up[:, FF:]
    sigmoid_gate = jax.nn.sigmoid(gate_part)
    swish_gate = gate_part * sigmoid_gate
    hidden = (swish_gate * up_part).astype(jnp.bfloat16)
    layer_output = (
        middle + last_product(hidden, lax.all_gather(shrink_weight, "shard", axis=0, tiled=True))
    ).astype(jnp.bfloat16)
    slope_hidden = fold_rows(cotangent, lax.all_gather(shrink_weight, "shard", axis=0, tiled=True))
    slope_gate = slope_hidden * up_part * (sigmoid_gate * (1.0 + gate_part * (1.0 - sigmoid_gate)))
    slope_up = slope_hidden * swish_gate
    slope_gate_up = jnp.concatenate([slope_gate, slope_up], axis=1).astype(jnp.bfloat16)
    slope_dense = last_product(
        slope_gate_up, lax.all_gather(expand_weight, "shard", axis=0, tiled=True)
    )
    dense_gain_part = jnp.sum(slope_dense * normed_two, axis=0)
    dense_shift_part = jnp.sum(slope_dense, axis=0)
    slope_middle = cotangent.astype(jnp.float32) + norm_backward(
        slope_dense, normed_two, inverse_two, gain_two
    )
    slope_branch = slope_middle.astype(jnp.bfloat16)
    slope_attended = fold_rows(
        slope_branch, lax.all_gather(output_weight, "shard", axis=0, tiled=True)
    )
    slope_attended = slope_attended.astype(jnp.bfloat16).reshape(token_count, HEADS, HEAD_DIM)
    probs_again = jnp.exp(score_block(queries, keys_all, allowed) - log_norm)
    weights_again = probs_again.astype(jnp.bfloat16)
    slope_values = jnp.einsum(
        "hts,thd->shd", weights_again, slope_attended, preferred_element_type=jnp.float32
    )
    slope_weights = jnp.einsum(
        "thd,shd->hts", slope_attended, values_all, preferred_element_type=jnp.float32
    )
    inner_part = jnp.sum(probs_again * slope_weights, axis=-1, keepdims=True)
    slope_scores = (probs_again * (slope_weights - inner_part)).astype(jnp.bfloat16)
    slope_queries = jnp.einsum(
        "hts,shd->thd", slope_scores, keys_all, preferred_element_type=jnp.float32
    ) * HEAD_DIM ** (-0.5)
    slope_keys = jnp.einsum(
        "hts,thd->shd", slope_scores, queries, preferred_element_type=jnp.float32
    ) * HEAD_DIM ** (-0.5)
    slope_joined = jnp.concatenate(
        [
            unrotate(slope_queries, cosines, sine_table).reshape(token_count, D),
            unrotate(slope_keys, cosines, sine_table).reshape(token_count, D),
            slope_values.reshape(token_count, D),
        ],
        axis=1,
    ).astype(jnp.bfloat16)
    bias_part = jnp.sum(slope_joined, axis=0, dtype=jnp.float32)
    slope_input = last_product(
        slope_joined, lax.all_gather(attend_weight, "shard", axis=0, tiled=True)
    )
    attend_gain_part = jnp.sum(slope_input * normed_one, axis=0)
    attend_shift_part = jnp.sum(slope_input, axis=0)
    tokens_gradient = (
        slope_middle + norm_backward(slope_input, normed_one, inverse_one, gain_one)
    ).astype(jnp.bfloat16)
    left_one = dense_input
    left_two = cotangent
    dense_owned = lax.psum_scatter(
        jnp.concatenate(
            [first_product(left_one, slope_gate_up), first_product(left_two, hidden)], axis=1
        ),
        "shard",
        scatter_dimension=0,
        tiled=True,
    )
    left_one = slope_branch
    left_two = attend_input
    attend_owned = lax.psum_scatter(
        jnp.concatenate(
            [first_product(left_one, attended), first_product(left_two, slope_joined)], axis=1
        ),
        "shard",
        scatter_dimension=0,
        tiled=True,
    )
    small_owned = (
        lax.psum_scatter(bias_part, "shard", scatter_dimension=0, tiled=True),
        lax.psum_scatter(attend_gain_part, "shard", scatter_dimension=0, tiled=True),
        lax.psum_scatter(attend_shift_part, "shard", scatter_dimension=0, tiled=True),
        lax.psum_scatter(dense_gain_part, "shard", scatter_dimension=0, tiled=True),
        lax.psum_scatter(dense_shift_part, "shard", scatter_dimension=0, tiled=True),
    )
    owned = (
        lax.psum(dense_owned.astype(jnp.bfloat16), "replica").astype(jnp.float32),
        lax.psum(attend_owned.astype(jnp.bfloat16), "replica").astype(jnp.float32),
        lax.psum(small_owned[0].astype(jnp.bfloat16), "replica").astype(jnp.float32),
        lax.psum(small_owned[1].astype(jnp.bfloat16), "replica").astype(jnp.float32),
        lax.psum(small_owned[2].astype(jnp.bfloat16), "replica").astype(jnp.float32),
        lax.psum(small_owned[3].astype(jnp.bfloat16), "replica").astype(jnp.float32),
        lax.psum(small_owned[4].astype(jnp.bfloat16), "replica").astype(jnp.float32),
    )
    dense_rows = owned[0]
    attend_rows = owned[1]
    return (
        layer_output,
        tokens_gradient,
        attend_rows[:, D:],
        owned[2],
        attend_rows[:, :D],
        owned[3],
        owned[4],
        dense_rows[:, : 2 * FF],
        dense_rows[:, 2 * FF :],
        owned[5],
        owned[6],
    )


def solution(mesh):
    in_specs = (
        P(("replica", "shard"), None),
        P(("replica", "shard"), None),
        P("shard", None),
        P("shard"),
        P("shard", None),
        P("shard"),
        P("shard"),
        P("shard", None),
        P("shard", None),
        P("shard"),
        P("shard"),
        P(("replica", "shard"), None),
    )
    out_specs = (
        P(("replica", "shard"), None),
        P(("replica", "shard"), None),
        P("shard", None),
        P("shard"),
        P("shard", None),
        P("shard"),
        P("shard"),
        P("shard", None),
        P("shard", None),
        P("shard"),
        P("shard"),
    )
    return jax.shard_map(shards, mesh=mesh, in_specs=in_specs, out_specs=out_specs, check_vma=False)
```

profile of v0, /device:TPU:0, one launch (start us, length us, event | category | flops | bytes accessed | tf_op | source)
XLA Modules:
  0.0 2805.3 jit_solution(7515153090226330550)
XLA Ops:
  10.1 23.0 all-gather
  33.2 17.3 all-gather.1
  50.5 18.7 all-gather.3
  69.3 17.3 all-gather.4
  86.6 19.3 all-gather.2
  107.0 34.2 %all-gather.10.cloned.1.call-done = bf16[2048,6144]{1,0:T(8,128)(2,1)} async-done(((bf16[128,6144]{1,0:T(8,128)(2,1)}), bf16[2048,6144]{1,0:T(8,128)(2,1)}) %all-gather.10.cloned.1.call-update) | async-done | bytes 25165840 | tf_op jit(solution)/shard_map/all_gather | solution.py:135
  141.2 13.8 convolution_add_fusion
  175.2 43.4 %all-gather.12.cloned.1.call-done = bf16[2048,2048]{1,0:T(8,128)(2,1)} async-done(((bf16[128,2048]{1,0:T(8,128)(2,1)}), bf16[2048,2048]{1,0:T(8,128)(2,1)}) %all-gather.12.cloned.1.call-update) | async-done | bytes 8388624 | tf_op jit(solution)/shard_map/all_gather | solution.py:155
  225.3 220.6 %all-gather.14.cloned.1.call-done = bf16[2048,11264]{1,0:T(8,128)(2,1)} async-done(((bf16[128,11264]{1,0:T(8,128)(2,1)}), bf16[2048,11264]{1,0:T(8,128)(2,1)}) %all-gather.14.cloned.1.call-update) | async-done | bytes 46137360 | tf_op jit(solution)/shard_map/all_gather | solution.py:159
  445.8 23.8 fusion.51
  469.6 96.4 %all-gather.16.cloned.1.call-done = bf16[2048,5632]{1,0:T(8,128)(2,1)} async-done(((bf16[128,5632]{1,0:T(8,128)(2,1)}), bf16[2048,5632]{1,0:T(8,128)(2,1)}) %all-gather.16.cloned.1.call-update) | async-done | bytes 23068688 | tf_op jit(solution)/shard_map/all_gather | solution.py:166
  566.0 17.0 multiply_convert_fusion.2
  583.0 22.2 multiply_reduce_fusion.1
  646.9 20.1 fusion.47
  667.0 44.1 %pad_maximum_fusion.1 = f32[2048,8192]{1,0:T(8,128)} fusion(f32[2048,6144]{1,0:T(8,128)} %fusion.47, f32[2048,2048]{1,0:T(8,128)} %fusion.31), kind=kLoop, calls=%fused_computation.1 | loop fusion | flops 16777216 | bytes 134217728 | tf_op jit(solution)/shard_map/concatenate | solution.py:231
  712.3 28.7 %convolution_bitcast_fusion = f32[2048,5632]{1,0:T(8,128)} fusion(bf16[256,5632]{1,0:T(8,128)(2,1)} %get-tuple-element.33, bf16[256,2048]{1,0:T(8,128)(2,1)S(1)} %copy-done.14), kind=kOutput, calls=%fused_computation.2 | convolution fusion | flops 5905580032 | bytes 50069504 | tf_op jit(solution)/shard_map/dot_general | solution.py:88
  741.0 55.7 %fusion.7 = f32[2048,11264]{1,0:T(8,128)} fusion(bf16[256,5632]{1,0:T(8,128)(2,1)} %get-tuple-element.32, bf16[256,5632]{1,0:T(8,128)(2,1)} %get-tuple-element.31, f32[256,2048]{1,0:T(8,128)S(1)} %copy-done.4, f32[2048]{0:T(1024)S(1)} %bitcast.84, f32[2048]{0:T(1024)S(1)} %bitcast.80, f32[256]{0:T(256)S(1)} %add_rsqrt_fusion, ...), kind=kOutput, calls=%fused_computation.22 | convolution fusion | flops 11825315840 | bytes 100157440 | tf_op jit(solution)/shard_map/dot_general | solution.py:88
  796.7 92.1 %pad_maximum_fusion = f32[2048,16896]{1,0:T(8,128)} fusion(f32[2048,5632]{1,0:T(8,128)} %convolution_bitcast_fusion, f32[2048,11264]{1,0:T(8,128)} %fusion.7), kind=kLoop, calls=%fused_computation | loop fusion | flops 34603008 | bytes 276824064 | tf_op jit(solution)/shard_map/concatenate | solution.py:221
  888.8 459.7 %reduce-scatter.3.cloned.1.call-done = f32[128,8192]{1,0:T(8,128)} async-done(((f32[2048,8192]{1,0:T(8,128)}), f32[128,8192]{1,0:T(8,128)}) %reduce-scatter.3.cloned.1.call-update) | async-done | bytes 4194320 | tf_op jit(solution)/shard_map/reduce_scatter | solution.py:230
  1352.2 1272.9 %reduce-scatter.5.cloned.1.call-done = f32[128,16896]{1,0:T(8,128)} async-done(((f32[2048,16896]{1,0:T(8,128)}), f32[128,16896]{1,0:T(8,128)}) %reduce-scatter.5.cloned.1.call-update) | async-done | bytes 8650768 | tf_op jit(solution)/shard_map/reduce_scatter | solution.py:220
  2636.1 14.3 fusion.24
  2650.5 60.8 %all-reduce.5 = (bf16[6144]{0:T(1024)(128)(2,1)S(1)}, bf16[2048]{0:T(1024)(128)(2,1)S(1)}, bf16[2048]{0:T(1024)(128)(2,1)S(1)}, bf16[2048]{0:T(1024)(128)(2,1)S(1)}, bf16[2048]{0:T(1024)(128)(2,1)S(1)}) all-reduce(f32[6144]{0:T(1024)S(1)} %convert_reduce_fusion, ...), channel_id=3, replica_groups=mesh['replica'=2,'shard'=16] {'shard'}, use_global_device_ids=true, to_apply=%region_15.16.clone | all-reduce | flops 14336 | bytes 86016
  2722.6 13.4 fusion.10
  2736.0 51.6 %all-reduce.10.cloned.1.call-done = (bf16[128,8192]{1,0:T(8,128)(2,1)}, bf16[128,16896]{1,0:T(8,128)(2,1)}) async-done(((bf16[128,8192]{1,0:T(8,128)(2,1)}, bf16[128,16896]{1,0:T(8,128)(2,1)}), (bf16[128,8192]{1,0:T(8,128)(2,1)}, bf16[128,16896]{1,0:T(8,128)(2,1)})) %all-reduce.10.cloned.1.call-update) | async-done | bytes 6422544 | tf_op jit(solution)/shard_map/psum | solution.py:247
  (187 shorter events, 108.6 us)
Async XLA Ops:
  7.2 26.0 copy-start.48
  7.2 43.3 %copy-start.49 = (bf16[128]{0:T(256)(128)(2,1)S(1)}, bf16[128]{0:T(256)(128)(2,1)}, u32[]{:S(2)}) copy-start(bf16[128]{0:T(256)(128)(2,1)} %param.21) | copy-start | bytes 772
  7.2 62.1 %copy-start.50 = (bf16[128]{0:T(256)(128)(2,1)S(1)}, bf16[128]{0:T(256)(128)(2,1)}, u32[]{:S(2)}) copy-start(bf16[128]{0:T(256)(128)(2,1)} %param.22) | copy-start | bytes 772
  7.2 98.7 %copy-start.43 = (s32[1,256]{1,0:T(1,128)S(1)}, s32[1,256]{1,0:T(1,128)}, u32[]{:S(2)}) copy-start(s32[1,256]{1,0:T(1,128)} %param.13) | copy-start | bytes 3076
  7.2 98.9 %copy-start.6 = (bf16[256,2048]{1,0:T(8,128)(2,1)S(1)}, bf16[256,2048]{1,0:T(8,128)(2,1)}, u32[]{:S(2)}) copy-start(bf16[256,2048]{1,0:T(8,128)(2,1)} %param.12) | copy-start | bytes 3145732
  7.3 134.0 %all-gather.10.cloned.1.call-start = ((), (), s32[]{:S(2)}) async-start(), calls=%async_computation.2 | async-start | bytes 26738688 | tf_op jit(solution)/shard_map/all_gather | solution.py:135
  8.0 210.6 %all-gather.12.cloned.1.call-start = ((), (), s32[]{:S(2)}) async-start(), calls=%async_computation.3 | async-start | bytes 8912896 | tf_op jit(solution)/shard_map/all_gather | solution.py:155
  8.7 437.1 %all-gather.14.cloned.1.call-start = ((), (), s32[]{:S(2)}) async-start(), calls=%async_computation.4 | async-start | bytes 49020928 | tf_op jit(solution)/shard_map/all_gather | solution.py:159
  9.5 556.6 %all-gather.16.cloned.1.call-start = ((), (), s32[]{:S(2)}) async-start(), calls=%async_computation.5 | async-start | bytes 24510464 | tf_op jit(solution)/shard_map/all_gather | solution.py:166
  10.0 1338.4 %reduce-scatter.3.cloned.1.call-start = ((), (), s32[]{:S(2)}) async-start(), calls=%async_computation.6 | async-start | bytes 71303168 | tf_op jit(solution)/shard_map/reduce_scatter | solution.py:230
  33.2 612.6 %copy-start.23 = (f32[16,1,128]{2,1,0:T(1,128)}, f32[16,1,128]{2,1,0:T(1,128)S(1)}, u32[]{:S(2)}) copy-start(f32[16,1,128]{2,1,0:T(1,128)S(1)} %convert_element_type.157) | copy-start | bytes 24580
  86.6 359.2 %copy-start.25 = (f32[16,1,128]{2,1,0:T(1,128)}, f32[16,1,128]{2,1,0:T(1,128)S(1)}, u32[]{:S(2)}) copy-start(f32[16,1,128]{2,1,0:T(1,128)S(1)} %convert_element_type.161) | copy-start | bytes 24580
  106.3 539.4 %copy-start.35 = (f32[256]{0:T(256)}, f32[256]{0:T(256)S(1)}, u32[]{:S(2)}) copy-start(f32[256]{0:T(256)S(1)} %broadcast_multiply_fusion.5) | copy-start | bytes 3076
  106.8 539.0 %copy-start.37 = (f32[256]{0:T(256)}, f32[256]{0:T(256)S(1)}, u32[]{:S(2)}) copy-start(f32[256]{0:T(256)S(1)} %add_rsqrt_fusion.1) | copy-start | bytes 3076
  106.9 57.6 %copy-start.39 = (f32[256,8]{0,1:T(8,128)}, f32[256,8]{0,1:T(8,128)S(1)}, u32[]{:S(2)}) copy-start(f32[256,8]{0,1:T(8,128)S(1)} %get-tuple-element.48) | copy-start | bytes 24580
  106.9 57.6 %copy-start.41 = (f32[256,8]{0,1:T(8,128)}, f32[256,8]{0,1:T(8,128)S(1)}, u32[]{:S(2)}) copy-start(f32[256,8]{0,1:T(8,128)S(1)} %get-tuple-element.49) | copy-start | bytes 24580
  224.8 358.2 %copy-start.3 = (f32[256,2048]{1,0:T(8,128)}, f32[256,2048]{1,0:T(8,128)S(1)}, u32[]{:S(2)}) copy-start(f32[256,2048]{1,0:T(8,128)S(1)} %get-tuple-element.53) | copy-start | bytes 6291460
  609.3 27.1 copy-start.1
  624.8 21.0 copy-start.15
  711.1 1914.0 %reduce-scatter.5.cloned.1.call-start = ((), (), s32[]{:S(2)}) async-start(), calls=%async_computation.7 | async-start | bytes 147062784 | tf_op jit(solution)/shard_map/reduce_scatter | solution.py:220
  712.3 28.7 %copy-start.4 = (f32[256,2048]{1,0:T(8,128)S(1)}, f32[256,2048]{1,0:T(8,128)}, u32[]{:S(2)}) copy-start(f32[256,2048]{1,0:T(8,128)} %copy-done.3) | copy-start | bytes 6291460
  712.3 28.7 %copy-start.26 = (f32[16,1,128]{2,1,0:T(1,128)S(1)}, f32[16,1,128]{2,1,0:T(1,128)}, u32[]{:S(2)}) copy-start(f32[16,1,128]{2,1,0:T(1,128)} %copy-done.25) | copy-start | bytes 24580
  888.7 1898.9 %all-reduce.10.cloned.1.call-start = ((), (), s32[]{:S(2)}) async-start(), calls=%async_computation.8 | async-start | bytes 12845056 | tf_op jit(solution)/shard_map/psum | solution.py:247
  2636.1 83.1 %copy-start.2 = (f32[256,2048]{1,0:T(8,128)S(1)}, f32[256,2048]{1,0:T(8,128)}, u32[]{:S(2)}) copy-start(f32[256,2048]{1,0:T(8,128)} %copy-done.1) | copy-start | bytes 6291460
  (37 other events, 138.0 us)
Sparse Core Ops, SparseCore 0:
  9.7 131.5 all-gather.9
  143.4 75.1 all-gather.11
  220.2 225.5 all-gather.13
  447.3 118.6 all-gather.15
  711.2 637.2 reduce-scatter.2
  1352.5 1272.4 reduce-scatter.4
  2631.1 156.4 all-reduce.9
where the time goes:
time: 2810 us
  waiting for transfers between devices  2180 us (78%)
  matrix products  251 us (9%)
  other arithmetic  165 us (6%)
  blocking collectives  161 us (6%)
  local copies, waits for them, and re-layouts  29.5 us (1%)
    reduce_scatter x1, waiting for transfers between devices, shards(): lax.psum_scatter(jnp.concatenate([first_product(left_one, slope_gate_up),...  1270 us
    reduce_scatter x1, waiting for transfers between devices, shards(): lax.psum_scatter(jnp.concatenate([first_product(left_one, attended), firs...  460 us
    all_gather x1, waiting for transfers between devices, shards(): lax.all_gather(expand_weight, 'shard', axis=0, tiled=True)  221 us
    dot_general x4, matrix products, first_product(): lax.dot_general(left_side, right_side, (((0,), (0,)), ((), ())), preferre...  113 us
    all_gather x1, waiting for transfers between devices, shards(): lax.all_gather(shrink_weight, 'shard', axis=0, tiled=True)  96.4 us
    concatenate x1, other arithmetic, shards(): jnp.concatenate([first_product(left_one, slope_gate_up), first_product(le...  92.1 us
    dot_general x4, matrix products, rows_product(): return jnp.dot(left_side, right_side, preferred_element_type=jnp.float32)  61.9 us
    unnamed x1, blocking collectives  60.8 us
  transfers between devices with their start and end apart: 7, of which 7 were waited for; matrix products, arithmetic and copies ran while one was open for 10% of the time, Pallas kernels for 0%

commit v1 on v0

v1 whole, which is shorter than its diff:
```python
import math

import jax
import jax.numpy as jnp
from jax import lax
from jax.experimental import pallas as pl
from jax.experimental.pallas import tpu as pltpu
from jax.sharding import Mesh
from jax.sharding import PartitionSpec as P

D = 2048
HEADS = 32
HEAD_DIM = 64
FF = 5632
ROT = 16
PARTS = 4
PART_HEADS = HEADS // PARTS
PART_D = D // PARTS
PART_FF = FF // PARTS

EPSILON = 1e-05
F32 = jnp.float32
BF16 = jnp.bfloat16
SWAP = [(0, 1), (1, 0)]
CORE_PIECES = 2
NO_COST = pl.CostEstimate(flops=0, bytes_accessed=0, transcendentals=0)


def over_x(value):
    return lax.ppermute(value, "x", SWAP)


def over_y(value):
    return lax.ppermute(value, "y", SWAP)


def near_start(block):
    half = block.shape[0] // 2
    return over_x(block[:half]), over_y(block[half:])


def near_end(block, arrived):
    half = block.shape[0] // 2
    return jnp.concatenate([block[:half], arrived[0]]), jnp.concatenate([block[half:], arrived[1]])


def gather_far(near):
    return over_y(near[0]), over_x(near[1])


def gather_tokens(block):
    near = near_end(block, near_start(block))
    return jnp.concatenate([*near, *gather_far(near)])


def scatter_first(far):
    half = far.shape[0] // 4
    return over_y(far[: 2 * half]), over_x(far[2 * half :])


def scatter_second(near, sent):
    half = near.shape[0] // 4
    low = near[: 2 * half] + sent[0].astype(F32)
    high = near[2 * half :] + sent[1].astype(F32)
    last = over_x(low[half:].astype(BF16)), over_y(high[half:].astype(BF16))
    return low[:half], high[:half], *last


def scatter_end(low, high, low_last, high_last):
    return jnp.concatenate([low + low_last.astype(F32), high + high_last.astype(F32)])


def scatter_product(left_side, right_side, product):
    count = left_side.shape[0] // 2
    far = product(left_side[count:], right_side)
    sent = scatter_first(far)
    near = product(after(left_side, far)[:count], right_side)
    return scatter_end(*scatter_second(near, after(sent, near)))


def transposed(flip):
    return [(y * 2 + c, (1 - c if flip else c) * 2 + y) for y in range(2) for c in range(2)]


def turned_back(flip):
    return [(target, source) for source, target in transposed(flip)]


def columns(weight, groups, part):
    width = weight.shape[1] // (groups * PARTS)
    return jnp.concatenate(
        [
            lax.dynamic_slice_in_dim(weight, (g * PARTS + part) * width, width, axis=1)
            for g in range(groups)
        ],
        axis=1,
    )


def turn_start(*weights_and_groups):
    x, c = lax.axis_index("x"), lax.axis_index("c")

    def part_of(part):
        return jnp.concatenate([columns(w, g, part) for w, g in weights_and_groups], axis=1)

    first = lax.ppermute(part_of(2 * x + c), ("y", "c"), transposed(False))
    second = lax.ppermute(part_of(2 * x + 1 - c), ("y", "c"), transposed(True))
    return first, second


def turn_end(first, second):
    straight = lax.axis_index("y") == 0
    return jnp.concatenate(
        [jnp.where(straight, first, second), jnp.where(straight, second, first)]
    )


def gather_pair(pair):
    return lax.all_gather(pair, ("z", "c"), axis=0, tiled=True)


def scatter_pair(partial):
    return lax.psum_scatter(partial, "z", scatter_dimension=0, tiled=True)


def core_columns(values, core):
    size = lax.axis_size("z")
    width = values.shape[1] // (2 * size)
    return jnp.concatenate(
        [
            lax.dynamic_slice_in_dim(values, (2 * i + core) * width, width, axis=1)
            for i in range(size)
        ],
        axis=1,
    )


def far_core(left_side, right_side):
    return core_product(left_side, right_side, 1 - lax.axis_index("c"))


def to_core(product, pieces):
    return [lax.ppermute(piece, "c", SWAP) for piece in jnp.split(product, pieces)]


def near_core(left_side, right_side, sent):
    return core_product(left_side, right_side, lax.axis_index("c"), sent)


def back_start(pair):
    rows = pair.shape[0] // 2
    upper, lower = pair[:rows], pair[rows:]
    straight = lax.axis_index("y") == 0
    first = lax.ppermute(jnp.where(straight, upper, lower), ("y", "c"), turned_back(False))
    second = lax.ppermute(jnp.where(straight, lower, upper), ("y", "c"), turned_back(True))
    return first, second


def back_end(first, second):
    straight = lax.axis_index("c") == 0
    return jnp.concatenate(
        [jnp.where(straight, first, second), jnp.where(straight, second, first)]
    )


def assemble(here, there, groups):
    rows = here.shape[0] // 2
    straight = lax.axis_index("x") == 0
    here = here[:rows], here[rows:]
    there = there[:rows], there[rows:]
    quarters = [jnp.where(straight, a, b) for a, b in zip(here, there)] + [
        jnp.where(straight, b, a) for a, b in zip(here, there)
    ]
    width = here[0].shape[1] // groups
    return jnp.concatenate(
        [q[:, g * width : (g + 1) * width] for g in range(groups) for q in quarters], axis=1
    ).astype(F32)


def norm_parts(values):
    center = jnp.mean(values, axis=-1, keepdims=True)
    centered = values - center
    variance = jnp.mean(centered * centered, axis=-1, keepdims=True)
    inverse = lax.rsqrt(variance + EPSILON)
    return (centered * inverse, inverse)


def norm_backward(slope, normed, inverse, gain_row):
    scaled = slope * gain_row
    first_mean = jnp.mean(scaled, axis=-1, keepdims=True)
    second_mean = jnp.mean(scaled * normed, axis=-1, keepdims=True)
    return inverse * (scaled - first_mean - normed * second_mean)


def rotary_tables(segment_all):
    length = segment_all.shape[1]
    places = jnp.arange(length)
    same_doc = segment_all[:, :, None] == segment_all[:, None, :]
    earlier = places[:, None] > places[None, :]
    position = jnp.sum(jnp.where(same_doc & earlier, 1.0, 0.0), axis=2).astype(F32)
    lane = jnp.arange(2 * HEAD_DIM) % HEAD_DIM
    frequency = jnp.exp((lane % (ROT // 2)).astype(F32) * (-2.0 * math.log(10000.0) / ROT))
    frequency = jnp.where(lane < ROT, frequency, 0.0)
    angles = position[:, :, None] * frequency
    sines = jnp.sin(angles)
    return (
        jnp.cos(angles),
        jnp.where(lane >= ROT // 2, sines, 0.0),
        jnp.where(lane < ROT // 2, -sines, 0.0),
    )


def rows_product(left_side, right_side):
    return jnp.dot(left_side, right_side, preferred_element_type=F32)


def last_product(left_side, right_side):
    return lax.dot_general(
        left_side, right_side, (((1,), (1,)), ((), ())), preferred_element_type=F32
    )


def first_product(left_side, right_side):
    return lax.dot_general(
        left_side, right_side, (((0,), (0,)), ((), ())), preferred_element_type=F32
    )


def turned(values, cosines, later, sooner):
    width = values.shape[1]
    copies = width // cosines.shape[1]
    wide = [jnp.concatenate([t] * copies, axis=1) for t in (cosines, later, sooner)]
    return (
        values * wide[0]
        + pltpu.roll(values, ROT // 2, 1) * wide[1]
        + pltpu.roll(values, width - ROT // 2, 1) * wide[2]
    )


def transposed_probs(queries, keys_all, allowed):
    scores = last_product(keys_all, queries) * HEAD_DIM ** (-0.5)
    scores = jnp.where(allowed, scores, -1e30)
    shifted = jnp.exp(scores - jnp.max(scores, axis=0, keepdims=True))
    return shifted * (1.0 / jnp.sum(shifted, axis=0, keepdims=True))


def allowed_pairs(segment_column, segment_row):
    length = segment_column.shape[0]
    source = lax.broadcasted_iota(jnp.int32, (length, length), 0)
    target = lax.broadcasted_iota(jnp.int32, (length, length), 1)
    return (segment_column == segment_row) & (source <= target)


def head(values, kind, h):
    start = kind * PART_D + h * HEAD_DIM
    return values[:, start : start + HEAD_DIM]


def sequence_rows(i, half):
    return (
        pl.ds(pl.multiple_of((i + 2 * (i // 2)) * half, half), half),
        pl.ds(pl.multiple_of((2 + 4 * (i % 2) + i // 2) * half, half), half),
    )


def read_rows(ref, places):
    return jnp.concatenate([ref[place] for place in places])


def write_rows(ref, places, value):
    half = value.shape[0] // 2
    ref[places[0]] = value[:half]
    ref[places[1]] = value[half:]


def attend_kernel(
    joined_ref, bias_ref, cos_ref, later_ref, sooner_ref, column_ref, row_ref, qkv_ref, out_ref
):
    count, _, rows = row_ref.shape

    @pl.loop(0, count)
    def _(i):
        places = sequence_rows(i, rows // 2)
        joined = read_rows(joined_ref, places) + bias_ref[...]
        tables = (cos_ref[i], later_ref[i], sooner_ref[i])
        qkv = jnp.concatenate(
            [
                turned(joined[:, :PART_D], *tables).astype(BF16),
                turned(joined[:, PART_D : 2 * PART_D], *tables).astype(BF16),
                joined[:, 2 * PART_D :].astype(BF16),
            ],
            axis=1,
        )
        qkv_ref[i] = qkv
        allowed = allowed_pairs(column_ref[i], row_ref[i])
        heads = []
        for h in range(PART_HEADS):
            weights = transposed_probs(head(qkv, 0, h), head(qkv, 1, h), allowed).astype(BF16)
            heads.append(first_product(weights, head(qkv, 2, h)))
        write_rows(out_ref, places, jnp.concatenate(heads, axis=1).astype(BF16))


def attend_back_kernel(
    qkv_ref, slope_ref, cos_ref, later_ref, sooner_ref, column_ref, row_ref, out_ref, bias_ref
):
    count, _, rows = row_ref.shape
    bias_ref[...] = jnp.zeros_like(bias_ref)

    @pl.loop(0, count)
    def _(i):
        places = sequence_rows(i, rows // 2)
        qkv, slope = qkv_ref[i], read_rows(slope_ref, places)
        tables = (cos_ref[i], -later_ref[i], -sooner_ref[i])
        allowed = allowed_pairs(column_ref[i], row_ref[i])
        slope_queries, slope_keys, slope_values = [], [], []
        for h in range(PART_HEADS):
            queries, keys_all, values_all = (head(qkv, kind, h) for kind in range(3))
            slope_here = head(slope, 0, h)
            probs = transposed_probs(queries, keys_all, allowed)
            slope_values.append(rows_product(probs.astype(BF16), slope_here))
            slope_weights = last_product(values_all, slope_here)
            inner = jnp.sum(probs * slope_weights, axis=0, keepdims=True)
            slope_scores = (probs * (slope_weights - inner)).astype(BF16)
            slope_keys.append(rows_product(slope_scores, queries) * HEAD_DIM ** (-0.5))
            slope_queries.append(first_product(slope_scores, keys_all) * HEAD_DIM ** (-0.5))
        joined = jnp.concatenate(
            [
                turned(jnp.concatenate(slope_queries, axis=1), *tables).astype(BF16),
                turned(jnp.concatenate(slope_keys, axis=1), *tables).astype(BF16),
                jnp.concatenate(slope_values, axis=1).astype(BF16),
            ],
            axis=1,
        )
        write_rows(out_ref, places, joined)
        bias_ref[...] += jnp.sum(joined.astype(F32), axis=0, keepdims=True)


def core_kernel(core_ref, left_ref, right_ref, *rest):
    product = first_product(left_ref[...], right_ref[...])
    out_ref = rest[-1]
    if len(rest) == 1:
        out_ref[...] = product.astype(BF16)
    width = out_ref.shape[0]
    starts = [(ref, at) for ref in rest[:-1] for at in range(0, ref.shape[0], width)]
    for step, (ref, at) in enumerate(starts):

        @pl.when(pl.program_id(0) == step)
        def _():
            out_ref[...] = (product + ref[pl.ds(at, width)].astype(F32)).astype(BF16)


def core_product(left_side, right_side, core, sent=None):
    steps = lax.axis_size("z")
    (tokens, features), count = left_side.shape, right_side.shape[1]
    width = features // (2 * steps)
    if width % 128:
        product = first_product(core_columns(left_side, core), right_side)
        if sent is not None:
            product = product + jnp.concatenate(sent).astype(F32)
        return product.astype(BF16)
    sent = sent or []
    whole = [
        pl.BlockSpec(piece.shape, lambda i, core: (0, 0), pipeline_mode=pl.Buffered(1))
        for piece in sent
    ]
    return pl.pallas_call(
        core_kernel,
        grid_spec=pltpu.PrefetchScalarGridSpec(
            num_scalar_prefetch=1,
            grid=(steps,),
            in_specs=[
                pl.BlockSpec((tokens, width), lambda i, core: (0, 2 * i + core[0])),
                pl.BlockSpec(
                    (tokens, count), lambda i, core: (0, 0), pipeline_mode=pl.Buffered(1)
                ),
            ]
            + whole,
            out_specs=pl.BlockSpec((width, count), lambda i, core: (i, 0)),
        ),
        out_shape=jax.ShapeDtypeStruct((features // 2, count), BF16),
        compiler_params=pltpu.CompilerParams(vmem_limit_bytes=40 * 2**20),
        cost_estimate=NO_COST,
    )(core[None].astype(jnp.int32), left_side, right_side, *sent)


def plain_kernel(left_ref, right_ref, out_ref):
    out_ref[...] = rows_product(left_ref[...], right_ref[...]).astype(out_ref.dtype)


def column_product(left_side, right_side, column, count, dtype):
    tokens, depth = left_side.shape
    rows = tokens // 2
    return pl.pallas_call(
        plain_kernel,
        grid=(2,),
        in_specs=[
            pl.BlockSpec((rows, depth), lambda i: (i, 0)),
            pl.BlockSpec((depth, count), lambda i: (0, column), pipeline_mode=pl.Buffered(1)),
        ],
        out_specs=pl.BlockSpec((rows, count), lambda i: (i, 0)),
        out_shape=jax.ShapeDtypeStruct((tokens, count), dtype),
        compiler_params=pltpu.CompilerParams(vmem_limit_bytes=40 * 2**20),
        cost_estimate=NO_COST,
    )(left_side, right_side)


def far_kernel(left_ref, right_ref, out_ref):
    out_ref[...] = last_product(left_ref[...], right_ref[...]).astype(out_ref.dtype)


def half_product(left_side, half, right_side, column, dtype):
    rows, depth = left_side.shape[0] // 2, left_side.shape[1]
    count = right_side.shape[0]
    tile = min(count, 256)
    return pl.pallas_call(
        far_kernel,
        grid=(count // tile,),
        in_specs=[
            pl.BlockSpec((rows, depth), lambda i: (half, 0)),
            pl.BlockSpec((tile, depth), lambda i: (i, column)),
        ],
        out_specs=pl.BlockSpec((rows, tile), lambda i: (0, i)),
        out_shape=jax.ShapeDtypeStruct((rows, count), dtype),
        compiler_params=pltpu.CompilerParams(vmem_limit_bytes=40 * 2**20),
        cost_estimate=NO_COST,
    )(left_side, right_side)


def slope_kernel(cotangent_ref, weight_ref, gate_ref, up_ref, out_ref):
    width = weight_ref.shape[1]
    for start in range(0, width, 256):
        here = pl.ds(start, min(256, width - start))
        slope = rows_product(cotangent_ref[...], weight_ref[:, here])
        gate, up = gate_ref[:, here], up_ref[:, here]
        sigmoid = 1.0 / (1.0 + jnp.exp(-gate))
        swish = gate * sigmoid
        out_ref[:, here] = (slope * up * (sigmoid * (1.0 + gate * (1.0 - sigmoid)))).astype(BF16)
        out_ref[:, pl.ds(width + start, here.size)] = (slope * swish).astype(BF16)


def slopes_of_gate_up(cotangent_all, weight, gate_up):
    (tokens, features), width = cotangent_all.shape, weight.shape[1]
    rows = tokens // 2
    return pl.pallas_call(
        slope_kernel,
        grid=(2,),
        in_specs=[
            pl.BlockSpec((rows, features), lambda i: (i, 0)),
            pl.BlockSpec((features, width), lambda i: (0, 0), pipeline_mode=pl.Buffered(1)),
            pl.BlockSpec((rows, width), lambda i: (i, 0)),
            pl.BlockSpec((rows, width), lambda i: (i, 1)),
        ],
        out_specs=pl.BlockSpec((rows, 2 * width), lambda i: (i, 0)),
        out_shape=jax.ShapeDtypeStruct((tokens, 2 * width), BF16),
        compiler_params=pltpu.CompilerParams(vmem_limit_bytes=48 * 2**20),
        cost_estimate=NO_COST,
    )(cotangent_all, weight, gate_up, gate_up)


def in_vmem(count):
    return [pl.BlockSpec(memory_space=pltpu.VMEM)] * count


def attend(joined, bias, tables, segment_all):
    count, rows = segment_all.shape
    return pl.pallas_call(
        attend_kernel,
        in_specs=in_vmem(7),
        out_specs=in_vmem(2),
        out_shape=[
            jax.ShapeDtypeStruct((count, rows, 3 * PART_D), BF16),
            jax.ShapeDtypeStruct((count * rows, PART_D), BF16),
        ],
        compiler_params=pltpu.CompilerParams(vmem_limit_bytes=48 * 2**20),
        cost_estimate=NO_COST,
    )(joined, bias[None], *tables, segment_all[:, :, None], segment_all[:, None])


def attend_back(qkv, slope, tables, segment_all):
    count, rows = segment_all.shape
    joined, bias = pl.pallas_call(
        attend_back_kernel,
        in_specs=in_vmem(7),
        out_specs=in_vmem(2),
        out_shape=[
            jax.ShapeDtypeStruct((count * rows, 3 * PART_D), BF16),
            jax.ShapeDtypeStruct((1, 3 * PART_D), F32),
        ],
        compiler_params=pltpu.CompilerParams(vmem_limit_bytes=48 * 2**20),
        cost_estimate=NO_COST,
    )(qkv, slope, *tables, segment_all[:, :, None], segment_all[:, None])
    return joined, bias[0]


def after(values, *others):
    return lax.optimization_barrier((values, others))[0]


def in_order(axis, own, other):
    straight = lax.axis_index(axis) == 0
    return jnp.where(straight, jnp.concatenate([own, other]), jnp.concatenate([other, own]))


def all_z_start(block):
    size = lax.axis_size("z")
    return [
        lax.ppermute(block, "z", [(i, (i + step) % size) for i in range(size)])
        for step in range(1, size)
    ]


def all_z_end(block, arrived):
    size, z = lax.axis_size("z"), lax.axis_index("z")
    whole = jnp.stack([block, *arrived])[::-1].astype(F32)
    return lax.dynamic_slice_in_dim(jnp.concatenate([whole, whole]), size - 1 - z, size, axis=0)


def small_sum(vector):
    z_size = lax.axis_size("z")
    for axis in ("c", "y", "x"):
        vector = vector + lax.ppermute(vector, axis, SWAP)
    step = 1
    while step < z_size:
        vector = vector + lax.ppermute(vector, "z", [(i, i ^ step) for i in range(z_size)])
        step *= 2
    return vector


def shards(
    tokens,
    segments,
    attend_weight,
    attend_bias,
    output_weight,
    attend_gain,
    attend_shift,
    expand_weight,
    shrink_weight,
    dense_gain,
    dense_shift,
    cotangent,
):
    x, y = lax.axis_index("x"), lax.axis_index("y")
    part = 2 * x + y

    vectors = [attend_bias, attend_gain, attend_shift, dense_gain, dense_shift]
    small = jnp.concatenate(vectors)[None]
    turned_first = turn_start((attend_weight, 3), (output_weight, 1))
    arrived = lax.ppermute(small, "c", SWAP), over_x(segments)
    turned_first, arrived = after((turned_first, arrived))

    attend_and_output = gather_pair(turn_end(*turned_first))
    attend_all = attend_and_output[:, : 3 * PART_D]
    small = in_order("c", small, arrived[0])
    segment_all = jnp.concatenate([segments, arrived[1]])
    tokens, small, segment_all = after((tokens, small, segment_all), turned_first)
    tokens_near = near_start(tokens)
    arrived = over_y(small), over_y(segment_all)
    tokens_near, arrived = after((tokens_near, arrived))

    tokens_near = near_end(tokens, tokens_near)
    small = in_order("y", small, arrived[0])
    segment_all = jnp.concatenate([segment_all, arrived[1]])
    tables = rotary_tables(segment_all)
    tokens_far = gather_far(tokens_near)
    turned_next = turn_start((after(expand_weight, tokens_near), 2))
    arrived = all_z_start(small)
    tokens_far, turned_next, arrived = after((tokens_far, turned_next, arrived))

    expand_all = gather_pair(turn_end(*turned_next))
    cotangent_near = near_start(after(cotangent, turned_next))
    turned_next = turn_start((after(shrink_weight, turned_next), 1))
    small = all_z_end(small, arrived)
    bounds = [0]
    for v in vectors:
        bounds.append(bounds[-1] + v.shape[0])
    bias_full, gain_one, shift_one, gain_two, shift_two = [
        small[:, :, i:j].reshape(-1) for i, j in zip(bounds, bounds[1:])
    ]
    bias_part = lax.dynamic_index_in_dim(
        bias_full.reshape(3, PARTS, PART_D), part, axis=1, keepdims=False
    ).reshape(-1)
    token_all = jnp.concatenate([*tokens_near, *tokens_far])
    normed_all, _ = norm_parts(token_all.astype(F32))
    attend_input = (normed_all * gain_one + shift_one).astype(BF16)

    joined = rows_product(attend_input, attend_all)
    cotangent_near, turned_next = after((cotangent_near, turned_next), joined)
    shrink_all = gather_pair(turn_end(*turned_next))
    cotangent_near = near_end(cotangent, cotangent_near)
    qkv, attended = attend(joined, bias_part, tables, segment_all)
    start_rows = tokens.astype(F32)
    count = attended.shape[0] // 2
    far = half_product(attended, 1, attend_and_output, 3, BF16)
    sent = scatter_first(far)
    near = half_product(after(attended, far), 0, attend_and_output, 3, F32)
    sent = after(sent, near)
    middle = start_rows + scatter_end(*scatter_second(near, sent))
    normed_two, inverse_two = norm_parts(middle)
    dense_input = gather_tokens((normed_two * gain_two + shift_two).astype(BF16))
    cotangent_far = gather_far(after(cotangent_near, dense_input))
    gate_up = rows_product(dense_input, expand_all)
    gate_part = gate_up[:, :PART_FF]
    up_part = gate_up[:, PART_FF:]
    sigmoid_gate = jax.nn.sigmoid(gate_part)
    swish_gate = gate_part * sigmoid_gate
    hidden = (swish_gate * up_part).astype(BF16)
    cotangent_far, hidden = after((cotangent_far, hidden))
    cotangent_all = jnp.concatenate([*cotangent_near, *cotangent_far])

    core_sent = to_core(far_core(cotangent_all, hidden), CORE_PIECES)
    shrink_partial = near_core(cotangent_all, hidden, core_sent)
    shrink_slopes = scatter_pair(shrink_partial)
    slope_gate_up = slopes_of_gate_up(after(cotangent_all, shrink_partial), shrink_all, gate_up)
    expand_far = far_core(dense_input, slope_gate_up)
    core_sent = to_core(expand_far, CORE_PIECES)
    far = half_product(after(slope_gate_up, expand_far), 1, expand_all, 0, BF16)
    sent = scatter_first(far)
    near = half_product(after(slope_gate_up, far), 0, expand_all, 0, F32)
    expand_partial = near_core(dense_input, after(slope_gate_up, near), core_sent)
    expand_partial, shrink_slopes = after((expand_partial, shrink_slopes))
    expand_slopes = scatter_pair(expand_partial)
    sent = after(sent, expand_partial)
    last = scatter_second(near, sent)
    slope_dense = scatter_end(*last)
    dense_gain_part = jnp.sum(slope_dense * normed_two, axis=0)
    dense_shift_part = jnp.sum(slope_dense, axis=0)
    slope_middle = cotangent.astype(F32) + norm_backward(
        slope_dense, normed_two, inverse_two, gain_two
    )
    slope_branch = slope_middle.astype(BF16)
    branch_near = near_start(slope_branch)
    output_far = half_product(after(hidden, slope_branch), 1, shrink_all, 0, BF16)
    branch_near = near_end(slope_branch, after(branch_near, output_far))
    branch_far = gather_far(branch_near)
    output_near = half_product(after(hidden, branch_near), 0, shrink_all, 0, F32)
    slope_branch = jnp.concatenate([*branch_near, *after(branch_far, output_near)])
    output_far, shrink_slopes = after((output_far, shrink_slopes), slope_branch)
    output_sent = scatter_first(output_far)
    shrink_turn = back_start(shrink_slopes)
    slope_attended = column_product(slope_branch, attend_and_output, 3, PART_D, BF16)
    slope_joined, bias_slope = attend_back(qkv, slope_attended, tables, segment_all)
    slope_joined, output_sent, shrink_turn = after((slope_joined, output_sent, shrink_turn))
    attend_far = far_core(attend_input, slope_joined)
    core_sent = to_core(attend_far, 1)
    far = half_product(after(slope_joined, attend_far), 1, attend_and_output, 0, BF16)
    sent = scatter_first(far)
    attend_partial = near_core(attend_input, after(slope_joined, far), core_sent)
    attend_partial, expand_slopes = after((attend_partial, expand_slopes))
    attend_slopes = scatter_pair(attend_partial)
    output_sent, shrink_turn = after((output_sent, shrink_turn), attend_partial)
    output_last = scatter_second(output_near, output_sent)
    shrink_here = back_end(*shrink_turn)
    shrink_there = over_x(shrink_here)
    near = half_product(after(slope_joined, attend_partial), 0, attend_and_output, 0, F32)
    sent, output_last, shrink_there = after((sent, output_last, shrink_there), near)
    layer_output = (middle + scatter_end(*output_last)).astype(BF16)
    last = scatter_second(near, sent)
    expand_turn = back_start(after(expand_slopes, near))
    output_core = far_core(after(slope_branch, near), attended)
    core_sent = to_core(output_core, 1)
    last, expand_turn, core_sent = after((last, expand_turn, core_sent), output_core)
    output_slopes = scatter_pair(near_core(slope_branch, attended, core_sent))
    expand_here = back_end(*expand_turn)
    expand_there = over_x(expand_here)
    shrink_gradient = assemble(shrink_here, shrink_there, 1)
    slope_input = scatter_end(*last)
    normed_one, inverse_one = norm_parts(start_rows)
    attend_gain_part = jnp.sum(slope_input * normed_one, axis=0)
    attend_shift_part = jnp.sum(slope_input, axis=0)
    tokens_gradient = (
        slope_middle + norm_backward(slope_input, normed_one, inverse_one, gain_one)
    ).astype(BF16)
    attend_slopes, expand_there = after((attend_slopes, expand_there), tokens_gradient)
    attend_turn = back_start(attend_slopes)
    expand_gradient = assemble(expand_here, expand_there, 2)
    attend_turn = after(attend_turn, expand_gradient)
    attend_here = back_end(*attend_turn)
    rows = attend_here.shape[0] // 2
    attend_there = over_x(attend_here[:rows])
    attend_there, output_slopes = after((attend_there, output_slopes))
    output_turn = back_start(output_slopes)
    attend_there = jnp.concatenate([attend_there, over_x(attend_here[rows:])])
    output_here = back_end(*output_turn)
    output_there = over_x(output_here)
    attend_gradient = assemble(attend_here, attend_there, 3)
    output_gradient = assemble(output_here, output_there, 1)

    bias_wide = lax.dynamic_update_slice(
        jnp.zeros((3, PARTS, PART_D), F32), bias_slope.reshape(3, 1, PART_D), (0, part, 0)
    ).reshape(-1)
    small = [bias_wide, attend_gain_part, attend_shift_part, dense_gain_part, dense_shift_part]
    total = small_sum(jnp.concatenate(small))
    index = (lax.axis_index("z") * 2 + y) * 2 + lax.axis_index("c")
    owned, at = [], 0
    for vector, own in zip(small, (attend_bias, attend_gain, attend_shift, dense_gain, dense_shift)):
        size = own.shape[0]
        owned.append(lax.dynamic_slice_in_dim(total, at + index * size, size))
        at += vector.shape[0]
    return (
        layer_output,
        tokens_gradient,
        attend_gradient,
        owned[0],
        output_gradient,
        owned[1],
        owned[2],
        expand_gradient,
        shrink_gradient,
        owned[3],
        owned[4],
    )


def solution(mesh):
    replicas, shard = mesh.shape["replica"], mesh.shape["shard"]
    cut = Mesh(mesh.devices.reshape(replicas, shard // 4, 2, 2), ("x", "z", "y", "c"))
    batch, owner = ("x", "z", "y", "c"), ("z", "y", "c")
    in_specs = (
        P(batch, None),
        P(batch, None),
        P(owner, None),
        P(owner),
        P(owner, None),
        P(owner),
        P(owner),
        P(owner, None),
        P(owner, None),
        P(owner),
        P(owner),
        P(batch, None),
    )
    out_specs = (
        P(batch, None),
        P(batch, None),
        P(owner, None),
        P(owner),
        P(owner, None),
        P(owner),
        P(owner),
        P(owner, None),
        P(owner, None),
        P(owner),
        P(owner),
    )
    return jax.shard_map(shards, mesh=cut, in_specs=in_specs, out_specs=out_specs, check_vma=False)
```

time: 2810 us -> 637 us (0.23)
  waiting for transfers between devices: 2180 us -> 221 us
  matrix products: 251 us -> 29 us
  blocking collectives: 161 us -> 0 us
  Pallas kernels: 0 us -> 152 us
  other arithmetic: 165 us -> 61.3 us
  starting transfers between devices: 0.27 us -> 83 us
  local copies, waits for them, and re-layouts: 29.5 us -> 67.6 us
    reduce_scatter x2 -> x4, waiting for transfers between devices: 1730 us -> 0.01 us  [scatter_pair(): return lax.psum_scatter(partial, 'z', scatter_dimension=0, tiled=True)]
    all_gather x4 -> x3, waiting for transfers between devices: 395 us -> 5.45 us  [gather_pair(): return lax.all_gather(pair, ('z', 'c'), axis=0, tiled=True)]
    dot_general x18 -> x2, matrix products: 251 us -> 29 us  [rows_product(): return jnp.dot(left_side, right_side, preferred_element_type=F32)]
    ppermute x0 -> x69, waiting for transfers between devices: none -> 215 us  [the longest x18 80.6 us: over_y(): return lax.ppermute(value, 'y', SWAP)]
    pallas_call x0 -> x20, Pallas kernels: none -> 152 us  [the longest x8 50.8 us: half_product(): pl.pallas_call(far_kernel, grid=(count // tile,), in_specs=[pl.BlockSpec(...]
    concatenate x4 -> x21, other arithmetic: 136 us -> 11.6 us  [the longest x4 3.45 us: near_end(): jnp.concatenate([block[:half], arrived[0]])]
    all_gather x5 -> x0, blocking collectives: 95.7 us -> none  [the longest x1 23 us: shards(): lax.all_gather(attend_gain, 'shard', axis=0, tiled=True)]
    ppermute x0 -> x69, starting transfers between devices: none -> 81.9 us  [the longest x22 23.7 us: over_x(): return lax.ppermute(value, 'x', SWAP)]
  transfers between devices with their start and end apart: 7 -> 76, of which waited for: 7 -> 38; matrix products, arithmetic and copies ran while one was open for 10% -> 21% of each run, Pallas kernels for 0% -> 24%
where the time goes in v1:
time: 637 us; the launch traced here: 630 us
  waiting for transfers between devices  221 us (35%)
  Pallas kernels  152 us (24%)
  starting transfers between devices  83 us (13%)
  local copies, waits for them, and re-layouts  67.6 us (11%)
  other arithmetic  61.3 us (10%)
  matrix products  29 us (5%)
  between operations  16.3 us (3%)
    ppermute x18, waiting for transfers between devices, over_y(): return lax.ppermute(value, 'y', SWAP)  80.6 us
    ppermute x22, waiting for transfers between devices, over_x(): return lax.ppermute(value, 'x', SWAP)  60.2 us
    pallas_call x8, Pallas kernels, half_product(): pl.pallas_call(far_kernel, grid=(count // tile,), in_specs=[pl.BlockSpec(...  50.8 us
    pallas_call x8, Pallas kernels, core_product(): pl.pallas_call(core_kernel, grid_spec=pltpu.PrefetchScalarGridSpec(num_sc...  50.2 us
    unnamed x188, local copies, waits for them, and re-layouts  38.7 us
    dot_general x2, matrix products, rows_product(): return jnp.dot(left_side, right_side, preferred_element_type=F32)  29 us
    ppermute x22, starting transfers between devices, over_x(): return lax.ppermute(value, 'x', SWAP)  23.7 us
    ppermute x3, waiting for transfers between devices, turn_start(): second = lax.ppermute(part_of(2 * x + 1 - c), ('y', 'c'), transposed(True))  22.7 us
  transfers between devices with their start and end apart: 76, of which 38 were waited for; matrix products, arithmetic and copies ran while one was open for 21% of the time, Pallas kernels for 24%

profile of v1, /device:TPU:0, one launch (start us, length us, event | category | flops | bytes accessed | tf_op | source)
XLA Modules:
  0.0 629.6 jit_solution(9937680478440487227)
XLA Ops:
  19.5 6.8 %collective-permute-done.1 = bf16[128,2048]{1,0:T(8,128)(2,1)S(1)} collective-permute-done((bf16[128,2048]{1,0:T(8,128)(2,1)S(1)}, bf16[128,2048]{1,0:T(8,128)(2,1)S(1)}, u32[]{:S(2)}, u32[]{:S(2)}) %collective-permute-start.1) | collective-permute-done | bytes 524320 | tf_op jit(solution)/shard_map/ppermute | solution.py:107
  35.0 10.0 %collective-permute-done.7 = s32[2,256]{1,0:T(2,128)S(1)} collective-permute-done((s32[2,256]{1,0:T(2,128)S(1)}, s32[2,256]{1,0:T(2,128)S(1)}, u32[]{:S(2)}, u32[]{:S(2)}) %collective-permute-start.7) | collective-permute-done | bytes 2080 | tf_op jit(solution)/shard_map/ppermute | solution.py:34
  56.6 6.6 %collective-permute-done.13 = bf16[4,896]{1,0:T(4,128)(2,1)S(1)} collective-permute-done((bf16[4,896]{1,0:T(4,128)(2,1)S(1)}, bf16[4,896]{1,0:T(4,128)(2,1)S(1)}, u32[]{:S(2)}, u32[]{:S(2)}) %collective-permute-start.13) | collective-permute-done | bytes 7200 | tf_op jit(solution)/shard_map/ppermute | solution.py:507
  67.0 15.9 %collective-permute-done.11 = bf16[128,2816]{1,0:T(8,128)(2,1)S(1)} collective-permute-done((bf16[128,2816]{1,0:T(8,128)(2,1)S(1)}, bf16[128,2816]{1,0:T(8,128)(2,1)S(1)}, u32[]{:S(2)}, u32[]{:S(2)}) %collective-permute-start.11) | collective-permute-done | bytes 720928 | tf_op jit(solution)/shard_map/ppermute | solution.py:107
  116.1 11.8 %fusion.6.joined_ref = f32[1024,1536]{1,0:T(8,128)} fusion(bf16[1024,2048]{1,0:T(8,128)(2,1)} %fusion.5.left_ref, bf16[2048,2048]{1,0:T(8,128)(2,1)} %all-gather.4.cloned.1.call-done.right_ref), kind=kOutput, calls=%fused_computation.8 | convolution fusion | flops 6442450944 | bytes 16777216 | tf_op jit(solution)/shard_map/dot_general | solution.py:214
  128.0 12.4 %shard_map.203 = (bf16[4,256,1536]{2,1,0:T(8,128)(2,1)}, bf16[1024,512]{1,0:T(8,128)(2,1)S(1)}) custom-call(f32[1024,1536]{1,0:T(8,128)} %fusion.6.joined_ref, f32[1,1536]{1,0:T(1,128)S(1)} %bitcast.24, f32[4,256,128]{2,1,0:T(8,128)S(1)} %get-tuple-element.310.cos_ref, f32[4,256,128]{2,1,0:T(8,128)S(1)} %get-tuple-element.309.later_ref, ...), custom_call_target="tpu_custom_call" | custom-call | tf_op jit(solution)/shard_map/pallas_call | solution.py:466
  152.4 16.9 %collective-permute-done.15 = bf16[256,2048]{1,0:T(8,128)(2,1)S(1)} collective-permute-done((bf16[256,2048]{1,0:T(8,128)(2,1)S(1)}, bf16[256,2048]{1,0:T(8,128)(2,1)S(1)}, u32[]{:S(2)}, u32[]{:S(2)}) %collective-permute-start.15) | collective-permute-done | bytes 1048608 | tf_op jit(solution)/shard_map/ppermute | solution.py:34
  176.0 7.8 %collective-permute-done.18 = bf16[128,2048]{1,0:T(8,128)(2,1)S(1)} collective-permute-done((bf16[128,2048]{1,0:T(8,128)(2,1)S(1)}, bf16[128,2048]{1,0:T(8,128)(2,1)S(1)}, u32[]{:S(2)}, u32[]{:S(2)}) %collective-permute-start.18) | collective-permute-done | bytes 524320 | tf_op jit(solution)/shard_map/ppermute | solution.py:34
  211.6 15.9 %collective-permute-done.25 = bf16[256,2048]{1,0:T(8,128)(2,1)S(1)} collective-permute-done((bf16[256,2048]{1,0:T(8,128)(2,1)S(1)}, bf16[256,2048]{1,0:T(8,128)(2,1)S(1)}, u32[]{:S(2)}, u32[]{:S(2)}) %collective-permute-start.25) | collective-permute-done | bytes 1048608 | tf_op jit(solution)/shard_map/ppermute | solution.py:34
  231.4 17.2 %fusion.51.gate_ref.up_ref = f32[1024,2816]{1,0:T(8,128)S(1)} fusion(bf16[1024,2048]{1,0:T(8,128)(2,1)} %constant_dynamic-update-slice_fusion.6.left_ref, bf16[2048,2816]{1,0:T(8,128)(2,1)} %all-gather.6.cloned.1.call-done.right_ref), kind=kOutput, calls=%fused_computation.243 | convolution fusion | flops 11811160064 | bytes 27262976 | tf_op jit(solution)/shard_map/dot_general | solution.py:214
  281.6 16.0 %shard_map.208.right_ref.left_ref = bf16[1024,2816]{1,0:T(8,128)(2,1)} custom-call(bf16[1024,2048]{1,0:T(8,128)(2,1)} %constant_dynamic-update-slice_fusion.12.left_ref.cotangent_ref, bf16[2048,1408]{1,0:T(8,128)(2,1)} %all-gather.8.cloned.1.call-done.weight_ref.right_ref, f32[1024,2816]{1,0:T(8,128)} %copy-done.21, f32[1024,2816]{1,0:T(8,128)} %copy-done.21), custom_call_target="tpu_custom_call" | custom-call | tf_op jit(solution)/shard_map/pallas_call | solution.py:444
  297.6 9.7 %shard_map.209 = bf16[1024,2816]{1,0:T(8,128)(2,1)S(1)} custom-call(s32[1]{0:T(128)} %bitcast.12.core_ref, bf16[1024,2048]{1,0:T(8,128)(2,1)} %constant_dynamic-update-slice_fusion.6.left_ref, bf16[1024,2816]{1,0:T(8,128)(2,1)} %shard_map.208.right_ref.left_ref), custom_call_target="tpu_custom_call" | custom-call | tf_op jit(solution)/shard_map/pallas_call | solution.py:366
  310.0 10.5 %shard_map.210 = bf16[512,2048]{1,0:T(8,128)(2,1)S(1)} custom-call(bf16[1024,2816]{1,0:T(8,128)(2,1)S(1)} %copy-done.2, bf16[2048,2816]{1,0:T(8,128)(2,1)} %all-gather.6.cloned.1.call-done.right_ref), custom_call_target="tpu_custom_call" | custom-call | tf_op jit(solution)/shard_map/pallas_call | solution.py:415
  325.1 10.6 %shard_map.211 = f32[512,2048]{1,0:T(8,128)S(1)} custom-call(bf16[1024,2816]{1,0:T(8,128)(2,1)S(1)} %copy-done.2, bf16[2048,2816]{1,0:T(8,128)(2,1)} %all-gather.6.cloned.1.call-done.right_ref), custom_call_target="tpu_custom_call" | custom-call | tf_op jit(solution)/shard_map/pallas_call | solution.py:415
  337.7 12.2 %shard_map.212 = bf16[1024,2816]{1,0:T(8,128)(2,1)} custom-call(s32[1]{0:T(128)} %bitcast.11.core_ref, bf16[1024,2048]{1,0:T(8,128)(2,1)} %constant_dynamic-update-slice_fusion.6.left_ref, bf16[1024,2816]{1,0:T(8,128)(2,1)} %shard_map.208.right_ref.left_ref, bf16[512,2816]{1,0:T(8,128)(2,1)S(1)} %collective-permute-done.33.rest_0_, ...), custom_call_target="tpu_custom_call" | custom-call | tf_op jit(solution)/shard_map/pallas_call | solution.py:366
  355.0 12.4 %collective-permute-done.36 = bf16[128,2048]{1,0:T(8,128)(2,1)S(1)} collective-permute-done((bf16[128,2048]{1,0:T(8,128)(2,1)S(1)}, bf16[128,2048]{1,0:T(8,128)(2,1)S(1)}, u32[]{:S(2)}, u32[]{:S(2)}) %collective-permute-start.36) | collective-permute-done | bytes 524320 | tf_op jit(solution)/shard_map/ppermute | solution.py:34
  396.6 12.3 %collective-permute-done.39 = bf16[256,2048]{1,0:T(8,128)(2,1)} collective-permute-done((bf16[256,2048]{1,0:T(8,128)(2,1)}, bf16[256,2048]{1,0:T(8,128)(2,1)}, u32[]{:S(2)}, u32[]{:S(2)}) %collective-permute-start.39) | collective-permute-done | bytes 1048608 | tf_op jit(solution)/shard_map/ppermute | solution.py:34
  421.9 19.6 %shard_map.216 = (bf16[1024,1536]{1,0:T(8,128)(2,1)}, f32[1,1536]{1,0:T(1,128)S(1)}) custom-call(bf16[4,256,1536]{2,1,0:T(8,128)(2,1)} %get-tuple-element.121.qkv_ref, bf16[1024,512]{1,0:T(8,128)(2,1)S(1)} %shard_map.215.slope_ref, f32[4,256,128]{2,1,0:T(8,128)S(1)} %copy-done.18, f32[4,256,128]{2,1,0:T(8,128)S(1)} %copy-done.16, ...), custom_call_target="tpu_custom_call" | custom-call | tf_op jit(solution)/shard_map/pallas_call | solution.py:481
  464.9 6.8 %shard_map.219 = bf16[1024,1536]{1,0:T(8,128)(2,1)S(1)} custom-call(s32[1]{0:T(128)} %bitcast.11.core_ref, bf16[1024,2048]{1,0:T(8,128)(2,1)S(1)} %copy-done.8, bf16[1024,1536]{1,0:T(8,128)(2,1)S(1)} %copy-done.4, bf16[1024,1536]{1,0:T(8,128)(2,1)} %collective-permute-done.47.rest_0_), custom_call_target="tpu_custom_call" | custom-call | tf_op jit(solution)/shard_map/pallas_call | solution.py:366
  484.6 8.1 %shard_map.220 = f32[512,2048]{1,0:T(8,128)S(1)} custom-call(bf16[1024,1536]{1,0:T(8,128)(2,1)S(1)} %copy-done.4, bf16[2048,2048]{1,0:T(8,128)(2,1)} %all-gather.4.cloned.1.call-done.right_ref), custom_call_target="tpu_custom_call" | custom-call | tf_op jit(solution)/shard_map/pallas_call | solution.py:415
  501.3 14.2 %collective-permute-done.50 = bf16[256,1408]{1,0:T(8,128)(2,1)S(1)} collective-permute-done((bf16[256,1408]{1,0:T(8,128)(2,1)S(1)}, bf16[256,1408]{1,0:T(8,128)(2,1)S(1)}, u32[]{:S(2)}, u32[]{:S(2)}) %collective-permute-start.50) | collective-permute-done | bytes 720928 | tf_op jit(solution)/shard_map/ppermute | solution.py:30
  522.3 8.6 %collective-permute-done.51 = bf16[128,2048]{1,0:T(8,128)(2,1)S(1)} collective-permute-done((bf16[128,2048]{1,0:T(8,128)(2,1)S(1)}, bf16[128,2048]{1,0:T(8,128)(2,1)S(1)}, u32[]{:S(2)}, u32[]{:S(2)}) %collective-permute-start.51) | collective-permute-done | bytes 524320 | tf_op jit(solution)/shard_map/ppermute | solution.py:30
  546.5 19.6 %collective-permute-done.63 = f32[14336]{0:T(1024)S(1)} collective-permute-done((f32[14336]{0:T(1024)S(1)}, f32[14336]{0:T(1024)S(1)}, u32[]{:S(2)}, u32[]{:S(2)}) %collective-permute-start.63) | collective-permute-done | bytes 57376 | tf_op jit(solution)/shard_map/ppermute | solution.py:521
  592.7 7.4 %collective-permute-done.59 = bf16[128,1536]{1,0:T(8,128)(2,1)S(1)} collective-permute-done((bf16[128,1536]{1,0:T(8,128)(2,1)S(1)}, bf16[128,1536]{1,0:T(8,128)(2,1)S(1)}, u32[]{:S(2)}, u32[]{:S(2)}) %collective-permute-start.59) | collective-permute-done | bytes 393248 | tf_op jit(solution)/shard_map/ppermute | solution.py:30
  (485 shorter events, 323.9 us)
Async XLA Ops:
  7.2 109.0 %all-gather.4.cloned.1.call-start = ((), (), s32[]{:S(2)}) async-start(), calls=%async_computation.4 | async-start | bytes 9437184 | tf_op jit(solution)/shard_map/all_gather | solution.py:119
  27.5 203.9 %all-gather.6.cloned.1.call-start = ((), (), s32[]{:S(2)}) async-start(), calls=%async_computation.5 | async-start | bytes 12976128 | tf_op jit(solution)/shard_map/all_gather | solution.py:119
  45.1 37.8 %collective-permute-start.8 = (bf16[256,2048]{1,0:T(8,128)(2,1)S(1)}, bf16[256,2048]{1,0:T(8,128)(2,1)S(1)}, u32[]{:S(2)}, u32[]{:S(2)}) collective-permute-start(bf16[256,2048]{1,0:T(8,128)(2,1)S(1)} %pad_maximum_fusion.4), channel_id=1, source_target_pairs={{0,2},{2,0},{1,3},{3,1},{4,6},{6,4},{5,7},{7,5},{8,10},{10,8},{9,1... | collective-permute-start | bytes 3145736 | tf_op jit(solution)/shard_map/ppermute | solution.py:34
  45.8 37.1 %collective-permute-start.9 = (bf16[256,2048]{1,0:T(8,128)(2,1)S(1)}, bf16[256,2048]{1,0:T(8,128)(2,1)}, u32[]{:S(2)}, u32[]{:S(2)}) collective-permute-start(bf16[256,2048]{1,0:T(8,128)(2,1)S(1)} %pad_maximum_fusion.5), channel_id=1, source_target_pairs={{0,16},{16,0},{1,17},{17,1},{2,18},{18,2},{3,19},{19,3},{4,20},{20... | collective-permute-start | bytes 3145736 | tf_op jit(solution)/shard_map/ppermute | solution.py:30
  47.3 35.6 %collective-permute-start.11 = (bf16[128,2816]{1,0:T(8,128)(2,1)S(1)}, bf16[128,2816]{1,0:T(8,128)(2,1)S(1)}, u32[]{:S(2)}, u32[]{:S(2)}) collective-permute-start(bf16[128,2816]{1,0:T(8,128)(2,1)S(1)} %pad_maximum_fusion.14), channel_id=1, source_target_pairs={{0,2},{1,0},{2,3},{3,1},{4,6},{5,4},{6,7},{7,5},{8,10},{9,8},{10,1... | collective-permute-start | bytes 2162696 | tf_op jit(solution)/shard_map/ppermute | solution.py:107
  85.1 196.5 %all-gather.8.cloned.1.call-start = ((), (), s32[]{:S(2)}) async-start(), calls=%async_computation.6 | async-start | bytes 6488064 | tf_op jit(solution)/shard_map/all_gather | solution.py:119
  94.8 51.4 %collective-permute-start.19 = (bf16[128,2048]{1,0:T(8,128)(2,1)}, bf16[128,2048]{1,0:T(8,128)(2,1)}, u32[]{:S(2)}, u32[]{:S(2)}) collective-permute-start(bf16[128,2048]{1,0:T(8,128)(2,1)} %get-tuple-element.266), channel_id=1, source_target_pairs={{0,16},{16,0},{1,17},{17,1},{2,18},{18,2},{3,19},{19,3},{4,20},{20... | collective-permute-start | bytes 1572872 | tf_op jit(solution)/shard_map/ppermute | solution.py:30
  95.7 50.6 %collective-permute-start.20 = (bf16[128,2048]{1,0:T(8,128)(2,1)}, bf16[128,2048]{1,0:T(8,128)(2,1)}, u32[]{:S(2)}, u32[]{:S(2)}) collective-permute-start(bf16[128,2048]{1,0:T(8,128)(2,1)} %get-tuple-element.265), channel_id=1, source_target_pairs={{0,2},{2,0},{1,3},{3,1},{4,6},{6,4},{5,7},{7,5},{8,10},{10,8},{9,1... | collective-permute-start | bytes 1572872 | tf_op jit(solution)/shard_map/ppermute | solution.py:34
  100.2 44.7 %collective-permute-start.21 = (bf16[128,1408]{1,0:T(8,128)(2,1)}, bf16[128,1408]{1,0:T(8,128)(2,1)}, u32[]{:S(2)}, u32[]{:S(2)}) collective-permute-start(bf16[128,1408]{1,0:T(8,128)(2,1)} %get-tuple-element.250), channel_id=1, source_target_pairs={{0,0},{1,2},{2,1},{3,3},{4,4},{5,6},{6,5},{7,7},{8,8},{9,10},{10,9... | collective-permute-start | bytes 1081352 | tf_op jit(solution)/shard_map/ppermute | solution.py:106
  104.8 41.5 %collective-permute-start.22 = (bf16[128,1408]{1,0:T(8,128)(2,1)}, bf16[128,1408]{1,0:T(8,128)(2,1)}, u32[]{:S(2)}, u32[]{:S(2)}) collective-permute-start(bf16[128,1408]{1,0:T(8,128)(2,1)} %get-tuple-element.249), channel_id=1, source_target_pairs={{0,2},{1,0},{2,3},{3,1},{4,6},{5,4},{6,7},{7,5},{8,10},{9,8},{10,1... | collective-permute-start | bytes 1081352 | tf_op jit(solution)/shard_map/ppermute | solution.py:107
  175.5 174.4 %reduce-scatter.5.cloned.1.call-start = ((), (), s32[]{:S(2)}) async-start(), calls=%async_computation.7 | async-start | bytes 3604480 | tf_op jit(solution)/shard_map/reduce_scatter | solution.py:123
  276.0 197.3 %reduce-scatter.7.cloned.1.call-start = ((), (), s32[]{:S(2)}) async-start(), calls=%async_computation.8 | async-start | bytes 7208960 | tf_op jit(solution)/shard_map/reduce_scatter | solution.py:123
  307.7 30.0 %collective-permute-start.33 = (bf16[512,2816]{1,0:T(8,128)(2,1)S(1)}, bf16[512,2816]{1,0:T(8,128)(2,1)S(1)}, u32[]{:S(2)}, u32[]{:S(2)}) collective-permute-start(bf16[512,2816]{1,0:T(8,128)(2,1)S(1)} %get-tuple-element.208), channel_id=1, source_target_pairs={{0,1},{1,0},{2,3},{3,2},{4,5},{5,4},{6,7},{7,6},{8,9},{9,8},{10,11... | collective-permute-start | bytes 8650760 | tf_op jit(solution)/shard_map/ppermute | solution.py:143
  308.1 29.6 %collective-permute-start.34 = (bf16[512,2816]{1,0:T(8,128)(2,1)S(1)}, bf16[512,2816]{1,0:T(8,128)(2,1)S(1)}, u32[]{:S(2)}, u32[]{:S(2)}) collective-permute-start(bf16[512,2816]{1,0:T(8,128)(2,1)S(1)} %get-tuple-element.207), channel_id=1, source_target_pairs={{0,1},{1,0},{2,3},{3,2},{4,5},{5,4},{6,7},{7,6},{8,9},{9,8},{10,11... | collective-permute-start | bytes 8650760 | tf_op jit(solution)/shard_map/ppermute | solution.py:143
  322.1 28.0 %collective-permute-start.31 = (bf16[256,2048]{1,0:T(8,128)(2,1)}, bf16[256,2048]{1,0:T(8,128)(2,1)}, u32[]{:S(2)}, u32[]{:S(2)}) collective-permute-start(bf16[256,2048]{1,0:T(8,128)(2,1)} %get-tuple-element.232), channel_id=1, source_target_pairs={{0,2},{2,0},{1,3},{3,1},{4,6},{6,4},{5,7},{7,5},{8,10},{10,8},{9,1... | collective-permute-start | bytes 3145736 | tf_op jit(solution)/shard_map/ppermute | solution.py:34
  349.9 223.3 %reduce-scatter.9.cloned.1.call-start = ((), (), s32[]{:S(2)}) async-start(), calls=%async_computation.9 | async-start | bytes 3932160 | tf_op jit(solution)/shard_map/reduce_scatter | solution.py:123
  413.8 29.3 %collective-permute-start.41 = (bf16[256,2048]{1,0:T(8,128)(2,1)S(1)}, bf16[256,2048]{1,0:T(8,128)(2,1)S(1)}, u32[]{:S(2)}, u32[]{:S(2)}) collective-permute-start(bf16[256,2048]{1,0:T(8,128)(2,1)S(1)} %get-tuple-element.230), channel_id=1, source_target_pairs={{0,2},{2,0},{1,3},{3,1},{4,6},{6,4},{5,7},{7,5},{8,10},{10,8},{9,1... | collective-permute-start | bytes 3145736 | tf_op jit(solution)/shard_map/ppermute | solution.py:34
  414.7 28.5 %collective-permute-start.42 = (bf16[256,2048]{1,0:T(8,128)(2,1)S(1)}, bf16[256,2048]{1,0:T(8,128)(2,1)S(1)}, u32[]{:S(2)}, u32[]{:S(2)}) collective-permute-start(bf16[256,2048]{1,0:T(8,128)(2,1)S(1)} %get-tuple-element.229), channel_id=1, source_target_pairs={{0,16},{16,0},{1,17},{17,1},{2,18},{18,2},{3,19},{19,3},{4,20},{20... | collective-permute-start | bytes 3145736 | tf_op jit(solution)/shard_map/ppermute | solution.py:30
  462.7 32.3 %collective-permute-start.45 = (bf16[256,2048]{1,0:T(8,128)(2,1)}, bf16[256,2048]{1,0:T(8,128)(2,1)}, u32[]{:S(2)}, u32[]{:S(2)}) collective-permute-start(bf16[256,2048]{1,0:T(8,128)(2,1)} %get-tuple-element.228), channel_id=1, source_target_pairs={{0,2},{2,0},{1,3},{3,1},{4,6},{6,4},{5,7},{7,5},{8,10},{10,8},{9,1... | collective-permute-start | bytes 3145736 | tf_op jit(solution)/shard_map/ppermute | solution.py:34
  463.8 32.0 %collective-permute-start.46 = (bf16[256,2048]{1,0:T(8,128)(2,1)}, bf16[256,2048]{1,0:T(8,128)(2,1)}, u32[]{:S(2)}, u32[]{:S(2)}) collective-permute-start(bf16[256,2048]{1,0:T(8,128)(2,1)} %get-tuple-element.227), channel_id=1, source_target_pairs={{0,16},{16,0},{1,17},{17,1},{2,18},{18,2},{3,19},{19,3},{4,20},{20... | collective-permute-start | bytes 3145736 | tf_op jit(solution)/shard_map/ppermute | solution.py:30
  480.6 112.1 %reduce-scatter.11.cloned.1.call-start = ((), (), s32[]{:S(2)}) async-start(), calls=%async_computation.10 | async-start | bytes 1310720 | tf_op jit(solution)/shard_map/reduce_scatter | solution.py:123
  483.8 31.8 %collective-permute-start.50 = (bf16[256,1408]{1,0:T(8,128)(2,1)S(1)}, bf16[256,1408]{1,0:T(8,128)(2,1)S(1)}, u32[]{:S(2)}, u32[]{:S(2)}) collective-permute-start(bf16[256,1408]{1,0:T(8,128)(2,1)S(1)} %pad_maximum_fusion.16), channel_id=1, source_target_pairs={{0,16},{16,0},{1,17},{17,1},{2,18},{18,2},{3,19},{19,3},{4,20},{20... | collective-permute-start | bytes 2162696 | tf_op jit(solution)/shard_map/ppermute | solution.py:30
  495.1 27.2 %collective-permute-start.53 = (bf16[128,2816]{1,0:T(8,128)(2,1)S(1)}, bf16[128,2816]{1,0:T(8,128)(2,1)S(1)}, u32[]{:S(2)}, u32[]{:S(2)}) collective-permute-start(bf16[128,2816]{1,0:T(8,128)(2,1)S(1)} %get-tuple-element.246), channel_id=1, source_target_pairs={{0,0},{2,1},{1,2},{3,3},{4,4},{6,5},{5,6},{7,7},{8,8},{10,9},{9,10... | collective-permute-start | bytes 2162696 | tf_op jit(solution)/shard_map/ppermute | solution.py:154
  533.2 39.9 %collective-permute-start.56 = (bf16[256,2816]{1,0:T(8,128)(2,1)}, bf16[256,2816]{1,0:T(8,128)(2,1)}, u32[]{:S(2)}, u32[]{:S(2)}) collective-permute-start(bf16[256,2816]{1,0:T(8,128)(2,1)} %pad_maximum_fusion.3), channel_id=1, source_target_pairs={{0,16},{16,0},{1,17},{17,1},{2,18},{18,2},{3,19},{19,3},{4,20},{20... | collective-permute-start | bytes 4325384 | tf_op jit(solution)/shard_map/ppermute | solution.py:30
  (125 other events, 1308.5 us)
Sparse Core Ops, SparseCore 0:
  27.6 84.8 all-gather.3
  114.1 106.4 all-gather.5
  222.9 58.7 all-gather.7
  284.3 54.8 reduce-scatter.4
  350.0 99.1 reduce-scatter.6
  480.7 57.4 reduce-scatter.8
  546.6 26.5 reduce-scatter.10

commit v2 on v1

--- a/solution.py
+++ b/solution.py
@@ -1,3 +1,4 @@
+import functools
 import math
 
 import jax
@@ -79,7 +80,12 @@
 
 
 def transposed(flip):
-    return [(y * 2 + c, (1 - c if flip else c) * 2 + y) for y in range(2) for c in range(2)]
+    pairs = [(y * 2 + c, (1 - c if flip else c) * 2 + y) for y in range(2) for c in range(2)]
+    return [pair for pair in pairs if pair[0] != pair[1]]
+
+
+def with_own(own, arrived):
+    return jnp.where(lax.axis_index("y") == lax.axis_index("c"), own, arrived)
 
 
 def turned_back(flip):
@@ -103,12 +109,14 @@
     def part_of(part):
         return jnp.concatenate([columns(w, g, part) for w, g in weights_and_groups], axis=1)
 
-    first = lax.ppermute(part_of(2 * x + c), ("y", "c"), transposed(False))
+    own = part_of(2 * x + c)
+    first = lax.ppermute(own, ("y", "c"), transposed(False))
     second = lax.ppermute(part_of(2 * x + 1 - c), ("y", "c"), transposed(True))
-    return first, second
-
-
-def turn_end(first, second):
+    return own, first, second
+
+
+def turn_end(own, first, second):
+    first = with_own(own, first)
     straight = lax.axis_index("y") == 0
     return jnp.concatenate(
         [jnp.where(straight, first, second), jnp.where(straight, second, first)]
@@ -151,12 +159,14 @@
     rows = pair.shape[0] // 2
     upper, lower = pair[:rows], pair[rows:]
     straight = lax.axis_index("y") == 0
-    first = lax.ppermute(jnp.where(straight, upper, lower), ("y", "c"), turned_back(False))
+    own = jnp.where(straight, upper, lower)
+    first = lax.ppermute(own, ("y", "c"), turned_back(False))
     second = lax.ppermute(jnp.where(straight, lower, upper), ("y", "c"), turned_back(True))
-    return first, second
-
-
-def back_end(first, second):
+    return own, first, second
+
+
+def back_end(own, first, second):
+    first = with_own(own, first)
     straight = lax.axis_index("c") == 0
     return jnp.concatenate(
         [jnp.where(straight, first, second), jnp.where(straight, second, first)]
@@ -383,6 +393,69 @@
     )(core[None].astype(jnp.int32), left_side, right_side, *sent)
 
 
+def near_and_core_kernel(
+    tiles, core_ref, left_ref, right_ref, other_ref, *refs
+):
+    step = pl.program_id(0)
+    near_ref, out_ref = refs[-2:]
+    width = out_ref.shape[0]
+
+    @pl.when(step < tiles)
+    def _():
+        near_ref[...] = last_product(left_ref[pl.ds(0, near_ref.shape[0])], right_ref[...])
+
+    starts = [(ref, at) for ref in refs[:-2] for at in range(0, ref.shape[0], width)]
+    for k, (ref, at) in enumerate(starts):
+
+        @pl.when(step == tiles + k)
+        def _():
+            product = first_product(other_ref[...], left_ref[...])
+            out_ref[...] = (product + ref[pl.ds(at, width)].astype(F32)).astype(BF16)
+
+
+def near_and_core(left_side, right_side, other, sent):
+    steps = lax.axis_size("z")
+    tokens, depth = left_side.shape
+    features, count = other.shape[1], right_side.shape[0]
+    width, tile = features // (2 * steps), min(count, 512)
+    if width % 128:
+        return half_product(left_side, 0, right_side, 0, F32), near_core(other, left_side, sent)
+    tiles = count // tile
+    once = pl.Buffered(1)
+    near, own = pl.pallas_call(
+        functools.partial(near_and_core_kernel, tiles),
+        grid_spec=pltpu.PrefetchScalarGridSpec(
+            num_scalar_prefetch=1,
+            grid=(tiles + steps,),
+            in_specs=[
+                pl.BlockSpec((tokens, depth), lambda i, core: (0, 0), pipeline_mode=once),
+                pl.BlockSpec((tile, depth), lambda i, core: (jnp.minimum(i, tiles - 1), 0)),
+                pl.BlockSpec(
+                    (tokens, width),
+                    lambda i, core: (0, 2 * jnp.maximum(i - tiles, 0) + core[0]),
+                ),
+            ]
+            + [
+                pl.BlockSpec(piece.shape, lambda i, core: (0, 0), pipeline_mode=once)
+                for piece in sent
+            ],
+            out_specs=[
+                pl.BlockSpec(
+                    (tokens // 2, tile), lambda i, core: (0, jnp.minimum(i, tiles - 1))
+                ),
+                pl.BlockSpec((width, depth), lambda i, core: (jnp.maximum(i - tiles, 0), 0)),
+            ],
+        ),
+        out_shape=[
+            jax.ShapeDtypeStruct((tokens // 2, count), F32),
+            jax.ShapeDtypeStruct((features // 2, depth), BF16),
+        ],
+        compiler_params=pltpu.CompilerParams(vmem_limit_bytes=44 * 2**20),
+        cost_estimate=NO_COST,
+    )(lax.axis_index("c")[None].astype(jnp.int32), left_side, right_side, other, *sent)
+    return near, own
+
+
 def plain_kernel(left_ref, right_ref, out_ref):
     out_ref[...] = rows_product(left_ref[...], right_ref[...]).astype(out_ref.dtype)
 
@@ -411,7 +484,7 @@
 def half_product(left_side, half, right_side, column, dtype):
     rows, depth = left_side.shape[0] // 2, left_side.shape[1]
     count = right_side.shape[0]
-    tile = min(count, 256)
+    tile = min(count, 512)
     return pl.pallas_call(
         far_kernel,
         grid=(count // tile,),
@@ -440,10 +513,10 @@
 
 def slopes_of_gate_up(cotangent_all, weight, gate_up):
     (tokens, features), width = cotangent_all.shape, weight.shape[1]
-    rows = tokens // 2
+    rows = tokens // 4
     return pl.pallas_call(
         slope_kernel,
-        grid=(2,),
+        grid=(4,),
         in_specs=[
             pl.BlockSpec((rows, features), lambda i: (i, 0)),
             pl.BlockSpec((features, width), lambda i: (0, 0), pipeline_mode=pl.Buffered(1)),
@@ -517,13 +590,13 @@
 
 def small_sum(vector):
     z_size = lax.axis_size("z")
-    for axis in ("c", "y", "x"):
+    for axis in ("c", "y"):
         vector = vector + lax.ppermute(vector, axis, SWAP)
     step = 1
     while step < z_size:
         vector = vector + lax.ppermute(vector, "z", [(i, i ^ step) for i in range(z_size)])
         step *= 2
-    return vector
+    return vector + over_x(vector)
 
 
 def shards(
@@ -616,8 +689,9 @@
     core_sent = to_core(expand_far, CORE_PIECES)
     far = half_product(after(slope_gate_up, expand_far), 1, expand_all, 0, BF16)
     sent = scatter_first(far)
-    near = half_product(after(slope_gate_up, far), 0, expand_all, 0, F32)
-    expand_partial = near_core(dense_input, after(slope_gate_up, near), core_sent)
+    near, expand_partial = near_and_core(
+        after(slope_gate_up, far), expand_all, dense_input, core_sent
+    )
     expand_partial, shrink_slopes = after((expand_partial, shrink_slopes))
     expand_slopes = scatter_pair(expand_partial)
     sent = after(sent, expand_partial)
@@ -641,30 +715,30 @@
     slope_attended = column_product(slope_branch, attend_and_output, 3, PART_D, BF16)
     slope_joined, bias_slope = attend_back(qkv, slope_attended, tables, segment_all)
     slope_joined, output_sent, shrink_turn = after((slope_joined, output_sent, shrink_turn))
+    shrink_here = back_end(*shrink_turn)
+    shrink_there = over_x(shrink_here)
     attend_far = far_core(attend_input, slope_joined)
     core_sent = to_core(attend_far, 1)
     far = half_product(after(slope_joined, attend_far), 1, attend_and_output, 0, BF16)
+    far, expand_slopes, core_sent = after((far, expand_slopes, core_sent))
+    expand_turn = back_start(expand_slopes)
     sent = scatter_first(far)
     attend_partial = near_core(attend_input, after(slope_joined, far), core_sent)
-    attend_partial, expand_slopes = after((attend_partial, expand_slopes))
     attend_slopes = scatter_pair(attend_partial)
-    output_sent, shrink_turn = after((output_sent, shrink_turn), attend_partial)
-    output_last = scatter_second(output_near, output_sent)
-    shrink_here = back_end(*shrink_turn)
-    shrink_there = over_x(shrink_here)
     near = half_product(after(slope_joined, attend_partial), 0, attend_and_output, 0, F32)
-    sent, output_last, shrink_there = after((sent, output_last, shrink_there), near)
-    layer_output = (middle + scatter_end(*output_last)).astype(BF16)
+    sent, expand_turn, shrink_there, near = after((sent, expand_turn, shrink_there, near))
     last = scatter_second(near, sent)
-    expand_turn = back_start(after(expand_slopes, near))
-    output_core = far_core(after(slope_branch, near), attended)
-    core_sent = to_core(output_core, 1)
-    last, expand_turn, core_sent = after((last, expand_turn, core_sent), output_core)
-    output_slopes = scatter_pair(near_core(slope_branch, attended, core_sent))
+    output_last = scatter_second(output_near, after(output_sent, near))
     expand_here = back_end(*expand_turn)
     expand_there = over_x(expand_here)
+    output_core = far_core(after(slope_branch, near), attended)
+    last, output_last = after((last, output_last), output_core)
+    core_sent = to_core(output_core, 1)
+    layer_output = (middle + scatter_end(*output_last)).astype(BF16)
     shrink_gradient = assemble(shrink_here, shrink_there, 1)
-    slope_input = scatter_end(*last)
+    output_partial = near_core(slope_branch, attended, core_sent)
+    output_slopes = scatter_pair(output_partial)
+    slope_input = scatter_end(*after(last, output_partial))
     normed_one, inverse_one = norm_parts(start_rows)
     attend_gain_part = jnp.sum(slope_input * normed_one, axis=0)
     attend_shift_part = jnp.sum(slope_input, axis=0)

time: 637 us -> 615 us (0.965)
  waiting for transfers between devices: 221 us -> 185 us
  Pallas kernels: 152 us -> 137 us
  starting transfers between devices: 83 us -> 92.7 us
  other arithmetic: 61.3 us -> 69.8 us
  local copies, waits for them, and re-layouts: 67.6 us -> 74.4 us
    ppermute x18, waiting for transfers between devices: 80.6 us -> 58.4 us  [over_y(): return lax.ppermute(value, 'y', SWAP)]
    ppermute x3 -> x2, waiting for transfers between devices: 22.1 us -> 3.02 us  [small_sum(): vector = vector + lax.ppermute(vector, axis, SWAP)]
    pallas_call x8 -> x7, Pallas kernels: 50.8 us -> 33 us  [half_product(): pl.pallas_call(far_kernel, grid=(count // tile,), in_specs=[pl.BlockSpec(...]
    pallas_call x1 -> x2, Pallas kernels: 16 us -> 33.8 us  [the longest x1 19.2 us: near_and_core(): pl.pallas_call(functools.partial(near_and_core_kernel, tiles), grid_spec=...]
    pallas_call x8 -> x7, Pallas kernels: 50.2 us -> 35.4 us  [core_product(): pl.pallas_call(core_kernel, grid_spec=pltpu.PrefetchScalarGridSpec(num_sc...]
    ppermute x2, waiting for transfers between devices: 1.13 us -> 12.8 us  [small_sum(): lax.ppermute(vector, 'z', [(i, i ^ step) for i in range(z_size)])]
    ppermute x22 -> x23, waiting for transfers between devices: 60.2 us -> 50.2 us  [over_x(): return lax.ppermute(value, 'x', SWAP)]
    ppermute x18, starting transfers between devices: 21 us -> 28.8 us  [over_y(): return lax.ppermute(value, 'y', SWAP)]
  transfers between devices with their start and end apart: 76 -> 76, of which waited for: 38 -> 35; matrix products, arithmetic and copies ran while one was open for 21% -> 24% of each run, Pallas kernels for 24% -> 23%
where the time goes in v2:
time: 615 us; the launch traced here: 604 us
  waiting for transfers between devices  185 us (30%)
  Pallas kernels  137 us (22%)
  starting transfers between devices  92.7 us (15%)
  local copies, waits for them, and re-layouts  74.4 us (12%)
  other arithmetic  69.8 us (11%)
  matrix products  29.4 us (5%)
  between operations  16.3 us (3%)
    ppermute x18, waiting for transfers between devices, over_y(): return lax.ppermute(value, 'y', SWAP)  58.4 us
    ppermute x23, waiting for transfers between devices, over_x(): return lax.ppermute(value, 'x', SWAP)  50.2 us
    unnamed x210, local copies, waits for them, and re-layouts  43 us
    pallas_call x7, Pallas kernels, core_product(): pl.pallas_call(core_kernel, grid_spec=pltpu.PrefetchScalarGridSpec(num_sc...  35.4 us
    pallas_call x7, Pallas kernels, half_product(): pl.pallas_call(far_kernel, grid=(count // tile,), in_specs=[pl.BlockSpec(...  33 us
    dot_general x2, matrix products, rows_product(): return jnp.dot(left_side, right_side, preferred_element_type=F32)  29.4 us
    ppermute x18, starting transfers between devices, over_y(): return lax.ppermute(value, 'y', SWAP)  28.8 us
    ppermute x3, waiting for transfers between devices, turn_start(): second = lax.ppermute(part_of(2 * x + 1 - c), ('y', 'c'), transposed(True))  25.5 us
  transfers between devices with their start and end apart: 76, of which 35 were waited for; matrix products, arithmetic and copies ran while one was open for 24% of the time, Pallas kernels for 23%

profile of v2, /device:TPU:0, one launch (start us, length us, event | category | flops | bytes accessed | tf_op | source)
XLA Modules:
  0.0 604.3 jit_solution(4486335991078230836)
XLA Ops:
  19.4 6.8 %collective-permute-done.1 = bf16[128,2048]{1,0:T(8,128)(2,1)S(1)} collective-permute-done((bf16[128,2048]{1,0:T(8,128)(2,1)S(1)}, bf16[128,2048]{1,0:T(8,128)(2,1)S(1)}, u32[]{:S(2)}, u32[]{:S(2)}) %collective-permute-start.1) | collective-permute-done | bytes 524320 | tf_op jit(solution)/shard_map/ppermute | solution.py:114
  35.0 8.8 %collective-permute-done.7 = s32[2,256]{1,0:T(2,128)S(1)} collective-permute-done((s32[2,256]{1,0:T(2,128)S(1)}, s32[2,256]{1,0:T(2,128)S(1)}, u32[]{:S(2)}, u32[]{:S(2)}) %collective-permute-start.7) | collective-permute-done | bytes 2080 | tf_op jit(solution)/shard_map/ppermute | solution.py:35
  65.7 18.7 %collective-permute-done.11 = bf16[128,2816]{1,0:T(8,128)(2,1)S(1)} collective-permute-done((bf16[128,2816]{1,0:T(8,128)(2,1)S(1)}, bf16[128,2816]{1,0:T(8,128)(2,1)S(1)}, u32[]{:S(2)}, u32[]{:S(2)}) %collective-permute-start.11) | collective-permute-done | bytes 720928 | tf_op jit(solution)/shard_map/ppermute | solution.py:114
  115.7 11.7 %fusion.6.joined_ref = f32[1024,1536]{1,0:T(8,128)} fusion(bf16[1024,2048]{1,0:T(8,128)(2,1)} %fusion.5.left_ref, bf16[2048,2048]{1,0:T(8,128)(2,1)} %all-gather.4.cloned.1.call-done.right_ref), kind=kOutput, calls=%fused_computation.8 | convolution fusion | flops 6442450944 | bytes 16777216 | tf_op jit(solution)/shard_map/dot_general | solution.py:224
  127.4 12.4 %shard_map.203 = (bf16[4,256,1536]{2,1,0:T(8,128)(2,1)}, bf16[1024,512]{1,0:T(8,128)(2,1)S(1)}) custom-call(f32[1024,1536]{1,0:T(8,128)} %fusion.6.joined_ref, f32[1,1536]{1,0:T(1,128)S(1)} %bitcast.24, f32[4,256,128]{2,1,0:T(8,128)S(1)} %get-tuple-element.328.cos_ref, f32[4,256,128]{2,1,0:T(8,128)S(1)} %get-tuple-element.327.later_ref, ...), custom_call_target="tpu_custom_call" | custom-call | tf_op jit(solution)/shard_map/pallas_call | solution.py:539
  150.1 16.5 %collective-permute-done.16 = bf16[256,2048]{1,0:T(8,128)(2,1)S(1)} collective-permute-done((bf16[256,2048]{1,0:T(8,128)(2,1)S(1)}, bf16[256,2048]{1,0:T(8,128)(2,1)S(1)}, u32[]{:S(2)}, u32[]{:S(2)}) %collective-permute-start.16) | collective-permute-done | bytes 1048608 | tf_op jit(solution)/shard_map/ppermute | solution.py:31
  173.9 7.4 %collective-permute-done.18 = bf16[128,2048]{1,0:T(8,128)(2,1)S(1)} collective-permute-done((bf16[128,2048]{1,0:T(8,128)(2,1)S(1)}, bf16[128,2048]{1,0:T(8,128)(2,1)S(1)}, u32[]{:S(2)}, u32[]{:S(2)}) %collective-permute-start.18) | collective-permute-done | bytes 524320 | tf_op jit(solution)/shard_map/ppermute | solution.py:35
  209.4 14.9 %collective-permute-done.25 = bf16[256,2048]{1,0:T(8,128)(2,1)S(1)} collective-permute-done((bf16[256,2048]{1,0:T(8,128)(2,1)S(1)}, bf16[256,2048]{1,0:T(8,128)(2,1)S(1)}, u32[]{:S(2)}, u32[]{:S(2)}) %collective-permute-start.25) | collective-permute-done | bytes 1048608 | tf_op jit(solution)/shard_map/ppermute | solution.py:35
  228.9 17.6 %fusion.51.gate_ref.up_ref = f32[1024,2816]{1,0:T(8,128)S(1)} fusion(bf16[1024,2048]{1,0:T(8,128)(2,1)} %constant_dynamic-update-slice_fusion.6.left_ref.other_ref, bf16[2048,2816]{1,0:T(8,128)(2,1)} %all-gather.6.cloned.1.call-done.right_ref), kind=kOutput, calls=%fused_computation.250 | convolution fusion | flops 11811160064 | bytes 27262976 | tf_op jit(solution)/shard_map/dot_general | solution.py:224
  266.2 5.7 shard_map.207
  273.8 7.8 %all-gather.8.cloned.1.call-done.weight_ref.right_ref = bf16[2048,1408]{1,0:T(8,128)(2,1)} async-done(((bf16[256,1408]{1,0:T(8,128)(2,1)}), bf16[2048,1408]{1,0:T(8,128)(2,1)}) %all-gather.8.cloned.1.call-update) | async-done | bytes 5767184 | tf_op jit(solution)/shard_map/all_gather | solution.py:127
  281.5 14.6 %shard_map.208.right_ref.left_ref = bf16[1024,2816]{1,0:T(8,128)(2,1)} custom-call(bf16[1024,2048]{1,0:T(8,128)(2,1)} %constant_dynamic-update-slice_fusion.12.left_ref.cotangent_ref, bf16[2048,1408]{1,0:T(8,128)(2,1)} %all-gather.8.cloned.1.call-done.weight_ref.right_ref, f32[1024,2816]{1,0:T(8,128)} %copy-done.24, f32[1024,2816]{1,0:T(8,128)} %copy-done.24), custom_call_target="tpu_custom_call" | custom-call | tf_op jit(solution)/shard_map/pallas_call | solution.py:517
  296.1 9.7 %shard_map.209 = bf16[1024,2816]{1,0:T(8,128)(2,1)S(1)} custom-call(s32[1]{0:T(128)} %bitcast.12.core_ref, bf16[1024,2048]{1,0:T(8,128)(2,1)} %constant_dynamic-update-slice_fusion.6.left_ref.other_ref, bf16[1024,2816]{1,0:T(8,128)(2,1)} %shard_map.208.right_ref.left_ref), custom_call_target="tpu_custom_call" | custom-call | tf_op jit(solution)/shard_map/pallas_call | solution.py:376
  309.6 8.8 %shard_map.210 = bf16[512,2048]{1,0:T(8,128)(2,1)S(1)} custom-call(bf16[1024,2816]{1,0:T(8,128)(2,1)S(1)} %copy-done.1, bf16[2048,2816]{1,0:T(8,128)(2,1)} %all-gather.6.cloned.1.call-done.right_ref), custom_call_target="tpu_custom_call" | custom-call | tf_op jit(solution)/shard_map/pallas_call | solution.py:488
  322.9 19.2 %shard_map.211 = (f32[512,2048]{1,0:T(8,128)S(1)}, bf16[1024,2816]{1,0:T(8,128)(2,1)}) custom-call(s32[1]{0:T(128)} %bitcast.9.core_ref, bf16[1024,2816]{1,0:T(8,128)(2,1)} %shard_map.208.right_ref.left_ref, bf16[2048,2816]{1,0:T(8,128)(2,1)} %all-gather.6.cloned.1.call-done.right_ref, ...), custom_call_target="tpu_custom_call" | custom-call | tf_op jit(solution)/shard_map/pallas_call | solution.py:425
  353.4 10.9 %collective-permute-done.36 = bf16[128,2048]{1,0:T(8,128)(2,1)S(1)} collective-permute-done((bf16[128,2048]{1,0:T(8,128)(2,1)S(1)}, bf16[128,2048]{1,0:T(8,128)(2,1)S(1)}, u32[]{:S(2)}, u32[]{:S(2)}) %collective-permute-start.36) | collective-permute-done | bytes 524320 | tf_op jit(solution)/shard_map/ppermute | solution.py:35
  374.5 6.3 %collective-permute-done.38 = bf16[128,2048]{1,0:T(8,128)(2,1)S(1)} collective-permute-done((bf16[128,2048]{1,0:T(8,128)(2,1)S(1)}, bf16[128,2048]{1,0:T(8,128)(2,1)S(1)}, u32[]{:S(2)}, u32[]{:S(2)}) %collective-permute-start.38) | collective-permute-done | bytes 524320 | tf_op jit(solution)/shard_map/ppermute | solution.py:35
  392.8 13.4 %collective-permute-done.40 = bf16[256,2048]{1,0:T(8,128)(2,1)} collective-permute-done((bf16[256,2048]{1,0:T(8,128)(2,1)}, bf16[256,2048]{1,0:T(8,128)(2,1)}, u32[]{:S(2)}, u32[]{:S(2)}) %collective-permute-start.40) | collective-permute-done | bytes 1048608 | tf_op jit(solution)/shard_map/ppermute | solution.py:31
  418.1 19.5 %shard_map.215 = (bf16[1024,1536]{1,0:T(8,128)(2,1)}, f32[1,1536]{1,0:T(1,128)S(1)}) custom-call(bf16[4,256,1536]{2,1,0:T(8,128)(2,1)} %get-tuple-element.131.qkv_ref, bf16[1024,512]{1,0:T(8,128)(2,1)S(1)} %shard_map.214.slope_ref, f32[4,256,128]{2,1,0:T(8,128)S(1)} %copy-done.18, f32[4,256,128]{2,1,0:T(8,128)S(1)} %copy-done.16, ...), custom_call_target="tpu_custom_call" | custom-call | tf_op jit(solution)/shard_map/pallas_call | solution.py:554
  476.2 6.7 %shard_map.219 = f32[512,2048]{1,0:T(8,128)S(1)} custom-call(bf16[1024,1536]{1,0:T(8,128)(2,1)S(1)} %copy-done.3, bf16[2048,2048]{1,0:T(8,128)(2,1)} %all-gather.4.cloned.1.call-done.right_ref), custom_call_target="tpu_custom_call" | custom-call | tf_op jit(solution)/shard_map/pallas_call | solution.py:488
  482.8 12.1 %collective-permute-done.49 = bf16[128,2816]{1,0:T(8,128)(2,1)} collective-permute-done((bf16[128,2816]{1,0:T(8,128)(2,1)}, bf16[128,2816]{1,0:T(8,128)(2,1)}, u32[]{:S(2)}, u32[]{:S(2)}) %collective-permute-start.49) | collective-permute-done | bytes 720928 | tf_op jit(solution)/shard_map/ppermute | solution.py:164
  498.3 8.0 %collective-permute-start.54 = (bf16[128,2048]{1,0:T(8,128)(2,1)S(1)}, bf16[128,2048]{1,0:T(8,128)(2,1)S(1)}, u32[]{:S(2)}, u32[]{:S(2)}) collective-permute-start(bf16[128,2048]{1,0:T(8,128)(2,1)S(1)} %slice.490), channel_id=1, source_target_pairs={{0,2},{2,0},{1,3},{3,1},{4,6},{6,4},{5,7},{7,5},{8,10},{10,8},{9,1... | collective-permute-start | bytes 1572872 | tf_op jit(solution)/shard_map/ppermute | solution.py:35
  544.3 7.5 %collective-permute-done.63 = f32[14336]{0:T(1024)S(1)} collective-permute-done((f32[14336]{0:T(1024)S(1)}, f32[14336]{0:T(1024)S(1)}, u32[]{:S(2)}, u32[]{:S(2)}) %collective-permute-start.63) | collective-permute-done | bytes 57376 | tf_op jit(solution)/shard_map/ppermute | solution.py:597
  581.4 7.0 %collective-permute-start.67 = (bf16[128,512]{1,0:T(8,128)(2,1)S(1)}, bf16[128,512]{1,0:T(8,128)(2,1)S(1)}, u32[]{:S(2)}, u32[]{:S(2)}) collective-permute-start(bf16[128,512]{1,0:T(8,128)(2,1)S(1)} %get-tuple-element.317), channel_id=1, source_target_pairs={{2,0},{0,1},{3,2},{1,3},{6,4},{4,5},{7,6},{5,7},{10,8},{8,9},{11,1... | collective-permute-start | bytes 393224 | tf_op jit(solution)/shard_map/ppermute | solution.py:164
  (506 shorter events, 316.0 us)
Async XLA Ops:
  7.2 108.5 %all-gather.4.cloned.1.call-start = ((), (), s32[]{:S(2)}) async-start(), calls=%async_computation.4 | async-start | bytes 9437184 | tf_op jit(solution)/shard_map/all_gather | solution.py:127
  27.4 201.4 %all-gather.6.cloned.1.call-start = ((), (), s32[]{:S(2)}) async-start(), calls=%async_computation.5 | async-start | bytes 12976128 | tf_op jit(solution)/shard_map/all_gather | solution.py:127
  43.9 40.5 %collective-permute-start.9 = (bf16[256,2048]{1,0:T(8,128)(2,1)S(1)}, bf16[256,2048]{1,0:T(8,128)(2,1)S(1)}, u32[]{:S(2)}, u32[]{:S(2)}) collective-permute-start(bf16[256,2048]{1,0:T(8,128)(2,1)S(1)} %pad_maximum_fusion.5), channel_id=1, source_target_pairs={{0,16},{16,0},{1,17},{17,1},{2,18},{18,2},{3,19},{19,3},{4,20},{20... | collective-permute-start | bytes 3145736 | tf_op jit(solution)/shard_map/ppermute | solution.py:31
  45.6 39.8 %collective-permute-start.8 = (bf16[256,2048]{1,0:T(8,128)(2,1)S(1)}, bf16[256,2048]{1,0:T(8,128)(2,1)}, u32[]{:S(2)}, u32[]{:S(2)}) collective-permute-start(bf16[256,2048]{1,0:T(8,128)(2,1)S(1)} %pad_maximum_fusion.4), channel_id=1, source_target_pairs={{0,2},{2,0},{1,3},{3,1},{4,6},{6,4},{5,7},{7,5},{8,10},{10,8},{9,1... | collective-permute-start | bytes 3145736 | tf_op jit(solution)/shard_map/ppermute | solution.py:35
  48.2 36.2 %collective-permute-start.11 = (bf16[128,2816]{1,0:T(8,128)(2,1)S(1)}, bf16[128,2816]{1,0:T(8,128)(2,1)S(1)}, u32[]{:S(2)}, u32[]{:S(2)}) collective-permute-start(bf16[128,2816]{1,0:T(8,128)(2,1)S(1)} %pad_maximum_fusion.14), channel_id=1, source_target_pairs={{0,2},{1,0},{2,3},{3,1},{4,6},{5,4},{6,7},{7,5},{8,10},{9,8},{10,1... | collective-permute-start | bytes 2162696 | tf_op jit(solution)/shard_map/ppermute | solution.py:114
  86.7 194.8 %all-gather.8.cloned.1.call-start = ((), (), s32[]{:S(2)}) async-start(), calls=%async_computation.6 | async-start | bytes 6488064 | tf_op jit(solution)/shard_map/all_gather | solution.py:127
  97.2 46.3 %collective-permute-start.22 = (bf16[128,1408]{1,0:T(8,128)(2,1)}, bf16[128,1408]{1,0:T(8,128)(2,1)}, u32[]{:S(2)}, u32[]{:S(2)}) collective-permute-start(bf16[128,1408]{1,0:T(8,128)(2,1)} %get-tuple-element.269), channel_id=1, source_target_pairs={{0,2},{1,0},{2,3},{3,1},{4,6},{5,4},{6,7},{7,5},{8,10},{9,8},{10,1... | collective-permute-start | bytes 1081352 | tf_op jit(solution)/shard_map/ppermute | solution.py:114
  99.8 44.9 %collective-permute-start.21 = (bf16[128,1408]{1,0:T(8,128)(2,1)}, bf16[128,1408]{1,0:T(8,128)(2,1)}, u32[]{:S(2)}, u32[]{:S(2)}) collective-permute-start(bf16[128,1408]{1,0:T(8,128)(2,1)} %get-tuple-element.145), channel_id=1, source_target_pairs={{1,2},{2,1},{5,6},{6,5},{9,10},{10,9},{13,14},{14,13},{17,18},{18,... | collective-permute-start | bytes 1081352 | tf_op jit(solution)/shard_map/ppermute | solution.py:113
  102.5 42.1 %collective-permute-start.20 = (bf16[128,2048]{1,0:T(8,128)(2,1)}, bf16[128,2048]{1,0:T(8,128)(2,1)}, u32[]{:S(2)}, u32[]{:S(2)}) collective-permute-start(bf16[128,2048]{1,0:T(8,128)(2,1)} %get-tuple-element.291), channel_id=1, source_target_pairs={{0,2},{2,0},{1,3},{3,1},{4,6},{6,4},{5,7},{7,5},{8,10},{10,8},{9,1... | collective-permute-start | bytes 1572872 | tf_op jit(solution)/shard_map/ppermute | solution.py:35
  103.6 41.0 %collective-permute-start.19 = (bf16[128,2048]{1,0:T(8,128)(2,1)}, bf16[128,2048]{1,0:T(8,128)(2,1)}, u32[]{:S(2)}, u32[]{:S(2)}) collective-permute-start(bf16[128,2048]{1,0:T(8,128)(2,1)} %get-tuple-element.292), channel_id=1, source_target_pairs={{0,16},{16,0},{1,17},{17,1},{2,18},{18,2},{3,19},{19,3},{4,20},{20... | collective-permute-start | bytes 1572872 | tf_op jit(solution)/shard_map/ppermute | solution.py:31
  173.4 170.7 %reduce-scatter.5.cloned.1.call-start = ((), (), s32[]{:S(2)}) async-start(), calls=%async_computation.7 | async-start | bytes 3604480 | tf_op jit(solution)/shard_map/reduce_scatter | solution.py:131
  273.6 183.1 %reduce-scatter.7.cloned.1.call-start = ((), (), s32[]{:S(2)}) async-start(), calls=%async_computation.8 | async-start | bytes 7208960 | tf_op jit(solution)/shard_map/reduce_scatter | solution.py:131
  319.9 25.6 %collective-permute-start.34 = (bf16[256,2048]{1,0:T(8,128)(2,1)}, bf16[256,2048]{1,0:T(8,128)(2,1)}, u32[]{:S(2)}, u32[]{:S(2)}) collective-permute-start(bf16[256,2048]{1,0:T(8,128)(2,1)} %get-tuple-element.253), channel_id=1, source_target_pairs={{0,16},{16,0},{1,17},{17,1},{2,18},{18,2},{3,19},{19,3},{4,20},{20... | collective-permute-start | bytes 3145736 | tf_op jit(solution)/shard_map/ppermute | solution.py:31
  344.2 218.5 %reduce-scatter.9.cloned.1.call-start = ((), (), s32[]{:S(2)}) async-start(), calls=%async_computation.9 | async-start | bytes 3932160 | tf_op jit(solution)/shard_map/reduce_scatter | solution.py:131
  410.5 27.1 %collective-permute-start.42 = (bf16[256,2048]{1,0:T(8,128)(2,1)}, bf16[256,2048]{1,0:T(8,128)(2,1)}, u32[]{:S(2)}, u32[]{:S(2)}) collective-permute-start(bf16[256,2048]{1,0:T(8,128)(2,1)} %get-tuple-element.251), channel_id=1, source_target_pairs={{0,16},{16,0},{1,17},{17,1},{2,18},{18,2},{3,19},{19,3},{4,20},{20... | collective-permute-start | bytes 3145736 | tf_op jit(solution)/shard_map/ppermute | solution.py:31
  448.5 34.3 %collective-permute-start.50 = (bf16[256,1408]{1,0:T(8,128)(2,1)}, bf16[256,1408]{1,0:T(8,128)(2,1)}, u32[]{:S(2)}, u32[]{:S(2)}) collective-permute-start(bf16[256,1408]{1,0:T(8,128)(2,1)} %pad_maximum_fusion.16), channel_id=1, source_target_pairs={{0,16},{16,0},{1,17},{17,1},{2,18},{18,2},{3,19},{19,3},{4,20},{20... | collective-permute-start | bytes 2162696 | tf_op jit(solution)/shard_map/ppermute | solution.py:31
  459.9 35.1 %collective-permute-start.47 = (bf16[256,2048]{1,0:T(8,128)(2,1)}, bf16[256,2048]{1,0:T(8,128)(2,1)}, u32[]{:S(2)}, u32[]{:S(2)}) collective-permute-start(bf16[256,2048]{1,0:T(8,128)(2,1)} %get-tuple-element.249), channel_id=1, source_target_pairs={{0,16},{16,0},{1,17},{17,1},{2,18},{18,2},{3,19},{19,3},{4,20},{20... | collective-permute-start | bytes 3145736 | tf_op jit(solution)/shard_map/ppermute | solution.py:31
  461.4 33.6 %collective-permute-start.46 = (bf16[256,2048]{1,0:T(8,128)(2,1)}, bf16[256,2048]{1,0:T(8,128)(2,1)}, u32[]{:S(2)}, u32[]{:S(2)}) collective-permute-start(bf16[256,2048]{1,0:T(8,128)(2,1)} %get-tuple-element.250), channel_id=1, source_target_pairs={{0,2},{2,0},{1,3},{3,1},{4,6},{6,4},{5,7},{7,5},{8,10},{10,8},{9,1... | collective-permute-start | bytes 3145736 | tf_op jit(solution)/shard_map/ppermute | solution.py:35
  465.3 29.7 %collective-permute-start.49 = (bf16[128,2816]{1,0:T(8,128)(2,1)}, bf16[128,2816]{1,0:T(8,128)(2,1)}, u32[]{:S(2)}, u32[]{:S(2)}) collective-permute-start(bf16[128,2816]{1,0:T(8,128)(2,1)} %get-tuple-element.267), channel_id=1, source_target_pairs={{2,0},{0,1},{3,2},{1,3},{6,4},{4,5},{7,6},{5,7},{10,8},{8,9},{11,1... | collective-permute-start | bytes 2162696 | tf_op jit(solution)/shard_map/ppermute | solution.py:164
  465.3 29.7 %collective-permute-start.48 = (bf16[128,2816]{1,0:T(8,128)(2,1)}, bf16[128,2816]{1,0:T(8,128)(2,1)}, u32[]{:S(2)}, u32[]{:S(2)}) collective-permute-start(bf16[128,2816]{1,0:T(8,128)(2,1)} %get-tuple-element.195), channel_id=1, source_target_pairs={{2,1},{1,2},{6,5},{5,6},{10,9},{9,10},{14,13},{13,14},{18,17},{17,... | collective-permute-start | bytes 2162696 | tf_op jit(solution)/shard_map/ppermute | solution.py:163
  475.7 100.7 %reduce-scatter.11.cloned.1.call-start = ((), (), s32[]{:S(2)}) async-start(), calls=%async_computation.10 | async-start | bytes 1310720 | tf_op jit(solution)/shard_map/reduce_scatter | solution.py:131
  497.8 26.4 %collective-permute-start.53 = (bf16[128,2048]{1,0:T(8,128)(2,1)S(1)}, bf16[128,2048]{1,0:T(8,128)(2,1)S(1)}, u32[]{:S(2)}, u32[]{:S(2)}) collective-permute-start(bf16[128,2048]{1,0:T(8,128)(2,1)S(1)} %slice.491), channel_id=1, source_target_pairs={{0,16},{16,0},{1,17},{17,1},{2,18},{18,2},{3,19},{19,3},{4,20},{20... | collective-permute-start | bytes 1572872 | tf_op jit(solution)/shard_map/ppermute | solution.py:31
  498.3 26.4 %collective-permute-start.54 = (bf16[128,2048]{1,0:T(8,128)(2,1)S(1)}, bf16[128,2048]{1,0:T(8,128)(2,1)S(1)}, u32[]{:S(2)}, u32[]{:S(2)}) collective-permute-start(bf16[128,2048]{1,0:T(8,128)(2,1)S(1)} %slice.490), channel_id=1, source_target_pairs={{0,2},{2,0},{1,3},{3,1},{4,6},{6,4},{5,7},{7,5},{8,10},{10,8},{9,1... | collective-permute-start | bytes 1572872 | tf_op jit(solution)/shard_map/ppermute | solution.py:35
  524.2 38.5 %collective-permute-start.56 = (bf16[256,2816]{1,0:T(8,128)(2,1)}, bf16[256,2816]{1,0:T(8,128)(2,1)}, u32[]{:S(2)}, u32[]{:S(2)}) collective-permute-start(bf16[256,2816]{1,0:T(8,128)(2,1)} %pad_maximum_fusion.3), channel_id=1, source_target_pairs={{0,16},{16,0},{1,17},{17,1},{2,18},{18,2},{3,19},{19,3},{4,20},{20... | collective-permute-start | bytes 4325384 | tf_op jit(solution)/shard_map/ppermute | solution.py:31
  (136 other events, 1268.1 us)
Sparse Core Ops, SparseCore 0:
  27.6 84.8 all-gather.3
  114.1 106.3 all-gather.5
  222.8 58.7 all-gather.7
  283.7 54.8 reduce-scatter.4
  344.3 99.4 reduce-scatter.6
  475.8 58.9 reduce-scatter.8
  539.6 27.1 reduce-scatter.10

commit v3 on v2

--- a/solution.py
+++ b/solution.py
@@ -462,10 +462,10 @@
 
 def column_product(left_side, right_side, column, count, dtype):
     tokens, depth = left_side.shape
-    rows = tokens // 2
+    rows = tokens // 4
     return pl.pallas_call(
         plain_kernel,
-        grid=(2,),
+        grid=(4,),
         in_specs=[
             pl.BlockSpec((rows, depth), lambda i: (i, 0)),
             pl.BlockSpec((depth, count), lambda i: (0, column), pipeline_mode=pl.Buffered(1)),
@@ -484,7 +484,7 @@
 def half_product(left_side, half, right_side, column, dtype):
     rows, depth = left_side.shape[0] // 2, left_side.shape[1]
     count = right_side.shape[0]
-    tile = min(count, 512)
+    tile = min(count, 512 if depth > PART_FF else 1024)
     return pl.pallas_call(
         far_kernel,
         grid=(count // tile,),

time: 615 us -> 616 us (level)
  transfers between devices with their start and end apart: 76 -> 76, of which waited for: 35 -> 35; matrix products, arithmetic and copies ran while one was open for 24% -> 24% of each run, Pallas kernels for 23% -> 22%
where the time goes in v3:
time: 616 us; the launch traced here: 605 us
  waiting for transfers between devices  187 us (30%)
  Pallas kernels  136 us (22%)
  starting transfers between devices  92.8 us (15%)
  local copies, waits for them, and re-layouts  74.4 us (12%)
  other arithmetic  69.8 us (11%)
  matrix products  29.5 us (5%)
  between operations  16.2 us (3%)
    ppermute x18, waiting for transfers between devices, over_y(): return lax.ppermute(value, 'y', SWAP)  58.9 us
    ppermute x23, waiting for transfers between devices, over_x(): return lax.ppermute(value, 'x', SWAP)  51.1 us
    unnamed x210, local copies, waits for them, and re-layouts  43 us
    pallas_call x7, Pallas kernels, core_product(): pl.pallas_call(core_kernel, grid_spec=pltpu.PrefetchScalarGridSpec(num_sc...  35.4 us
    pallas_call x7, Pallas kernels, half_product(): pl.pallas_call(far_kernel, grid=(count // tile,), in_specs=[pl.BlockSpec(...  31.5 us
    dot_general x2, matrix products, rows_product(): return jnp.dot(left_side, right_side, preferred_element_type=F32)  29.5 us
    ppermute x18, starting transfers between devices, over_y(): return lax.ppermute(value, 'y', SWAP)  28.4 us
    ppermute x3, waiting for transfers between devices, turn_start(): second = lax.ppermute(part_of(2 * x + 1 - c), ('y', 'c'), transposed(True))  25.5 us
  transfers between devices with their start and end apart: 76, of which 35 were waited for; matrix products, arithmetic and copies ran while one was open for 24% of the time, Pallas kernels for 22%

profile of v3, /device:TPU:0, one launch (start us, length us, event | category | flops | bytes accessed | tf_op | source)
XLA Modules:
  0.0 604.8 jit_solution(1074138390778730123)
XLA Ops:
  19.4 6.8 %collective-permute-done.1 = bf16[128,2048]{1,0:T(8,128)(2,1)S(1)} collective-permute-done((bf16[128,2048]{1,0:T(8,128)(2,1)S(1)}, bf16[128,2048]{1,0:T(8,128)(2,1)S(1)}, u32[]{:S(2)}, u32[]{:S(2)}) %collective-permute-start.1) | collective-permute-done | bytes 524320 | tf_op jit(solution)/shard_map/ppermute | solution.py:114
  35.0 8.8 %collective-permute-done.7 = s32[2,256]{1,0:T(2,128)S(1)} collective-permute-done((s32[2,256]{1,0:T(2,128)S(1)}, s32[2,256]{1,0:T(2,128)S(1)}, u32[]{:S(2)}, u32[]{:S(2)}) %collective-permute-start.7) | collective-permute-done | bytes 2080 | tf_op jit(solution)/shard_map/ppermute | solution.py:35
  65.7 18.7 %collective-permute-done.11 = bf16[128,2816]{1,0:T(8,128)(2,1)S(1)} collective-permute-done((bf16[128,2816]{1,0:T(8,128)(2,1)S(1)}, bf16[128,2816]{1,0:T(8,128)(2,1)S(1)}, u32[]{:S(2)}, u32[]{:S(2)}) %collective-permute-start.11) | collective-permute-done | bytes 720928 | tf_op jit(solution)/shard_map/ppermute | solution.py:114
  115.6 11.7 %fusion.6.joined_ref = f32[1024,1536]{1,0:T(8,128)} fusion(bf16[1024,2048]{1,0:T(8,128)(2,1)} %fusion.5.left_ref, bf16[2048,2048]{1,0:T(8,128)(2,1)} %all-gather.4.cloned.1.call-done.right_ref), kind=kOutput, calls=%fused_computation.8 | convolution fusion | flops 6442450944 | bytes 16777216 | tf_op jit(solution)/shard_map/dot_general | solution.py:224
  127.4 12.4 %shard_map.203 = (bf16[4,256,1536]{2,1,0:T(8,128)(2,1)}, bf16[1024,512]{1,0:T(8,128)(2,1)S(1)}) custom-call(f32[1024,1536]{1,0:T(8,128)} %fusion.6.joined_ref, f32[1,1536]{1,0:T(1,128)S(1)} %bitcast.24, f32[4,256,128]{2,1,0:T(8,128)S(1)} %get-tuple-element.328.cos_ref, f32[4,256,128]{2,1,0:T(8,128)S(1)} %get-tuple-element.327.later_ref, ...), custom_call_target="tpu_custom_call" | custom-call | tf_op jit(solution)/shard_map/pallas_call | solution.py:539
  149.2 16.9 %collective-permute-done.16 = bf16[256,2048]{1,0:T(8,128)(2,1)S(1)} collective-permute-done((bf16[256,2048]{1,0:T(8,128)(2,1)S(1)}, bf16[256,2048]{1,0:T(8,128)(2,1)S(1)}, u32[]{:S(2)}, u32[]{:S(2)}) %collective-permute-start.16) | collective-permute-done | bytes 1048608 | tf_op jit(solution)/shard_map/ppermute | solution.py:31
  173.3 7.6 %collective-permute-done.18 = bf16[128,2048]{1,0:T(8,128)(2,1)S(1)} collective-permute-done((bf16[128,2048]{1,0:T(8,128)(2,1)S(1)}, bf16[128,2048]{1,0:T(8,128)(2,1)S(1)}, u32[]{:S(2)}, u32[]{:S(2)}) %collective-permute-start.18) | collective-permute-done | bytes 524320 | tf_op jit(solution)/shard_map/ppermute | solution.py:35
  209.0 15.0 %collective-permute-done.25 = bf16[256,2048]{1,0:T(8,128)(2,1)S(1)} collective-permute-done((bf16[256,2048]{1,0:T(8,128)(2,1)S(1)}, bf16[256,2048]{1,0:T(8,128)(2,1)S(1)}, u32[]{:S(2)}, u32[]{:S(2)}) %collective-permute-start.25) | collective-permute-done | bytes 1048608 | tf_op jit(solution)/shard_map/ppermute | solution.py:35
  228.5 17.7 %fusion.51.gate_ref.up_ref = f32[1024,2816]{1,0:T(8,128)S(1)} fusion(bf16[1024,2048]{1,0:T(8,128)(2,1)} %constant_dynamic-update-slice_fusion.6.left_ref.other_ref, bf16[2048,2816]{1,0:T(8,128)(2,1)} %all-gather.6.cloned.1.call-done.right_ref), kind=kOutput, calls=%fused_computation.250 | convolution fusion | flops 11811160064 | bytes 27262976 | tf_op jit(solution)/shard_map/dot_general | solution.py:224
  265.8 5.7 shard_map.207
  273.7 7.8 %all-gather.8.cloned.1.call-done.weight_ref.right_ref = bf16[2048,1408]{1,0:T(8,128)(2,1)} async-done(((bf16[256,1408]{1,0:T(8,128)(2,1)}), bf16[2048,1408]{1,0:T(8,128)(2,1)}) %all-gather.8.cloned.1.call-update) | async-done | bytes 5767184 | tf_op jit(solution)/shard_map/all_gather | solution.py:127
  281.5 14.6 %shard_map.208.right_ref.left_ref = bf16[1024,2816]{1,0:T(8,128)(2,1)} custom-call(bf16[1024,2048]{1,0:T(8,128)(2,1)} %constant_dynamic-update-slice_fusion.12.left_ref.cotangent_ref, bf16[2048,1408]{1,0:T(8,128)(2,1)} %all-gather.8.cloned.1.call-done.weight_ref.right_ref, f32[1024,2816]{1,0:T(8,128)} %copy-done.24, f32[1024,2816]{1,0:T(8,128)} %copy-done.24), custom_call_target="tpu_custom_call" | custom-call | tf_op jit(solution)/shard_map/pallas_call | solution.py:517
  296.1 9.7 %shard_map.209 = bf16[1024,2816]{1,0:T(8,128)(2,1)S(1)} custom-call(s32[1]{0:T(128)} %bitcast.12.core_ref, bf16[1024,2048]{1,0:T(8,128)(2,1)} %constant_dynamic-update-slice_fusion.6.left_ref.other_ref, bf16[1024,2816]{1,0:T(8,128)(2,1)} %shard_map.208.right_ref.left_ref), custom_call_target="tpu_custom_call" | custom-call | tf_op jit(solution)/shard_map/pallas_call | solution.py:376
  309.6 8.8 %shard_map.210 = bf16[512,2048]{1,0:T(8,128)(2,1)S(1)} custom-call(bf16[1024,2816]{1,0:T(8,128)(2,1)S(1)} %copy-done.1, bf16[2048,2816]{1,0:T(8,128)(2,1)} %all-gather.6.cloned.1.call-done.right_ref), custom_call_target="tpu_custom_call" | custom-call | tf_op jit(solution)/shard_map/pallas_call | solution.py:488
  322.9 19.2 %shard_map.211 = (f32[512,2048]{1,0:T(8,128)S(1)}, bf16[1024,2816]{1,0:T(8,128)(2,1)}) custom-call(s32[1]{0:T(128)} %bitcast.9.core_ref, bf16[1024,2816]{1,0:T(8,128)(2,1)} %shard_map.208.right_ref.left_ref, bf16[2048,2816]{1,0:T(8,128)(2,1)} %all-gather.6.cloned.1.call-done.right_ref, ...), custom_call_target="tpu_custom_call" | custom-call | tf_op jit(solution)/shard_map/pallas_call | solution.py:425
  353.4 10.9 %collective-permute-done.36 = bf16[128,2048]{1,0:T(8,128)(2,1)S(1)} collective-permute-done((bf16[128,2048]{1,0:T(8,128)(2,1)S(1)}, bf16[128,2048]{1,0:T(8,128)(2,1)S(1)}, u32[]{:S(2)}, u32[]{:S(2)}) %collective-permute-start.36) | collective-permute-done | bytes 524320 | tf_op jit(solution)/shard_map/ppermute | solution.py:35
  374.1 6.6 %collective-permute-done.38 = bf16[128,2048]{1,0:T(8,128)(2,1)S(1)} collective-permute-done((bf16[128,2048]{1,0:T(8,128)(2,1)S(1)}, bf16[128,2048]{1,0:T(8,128)(2,1)S(1)}, u32[]{:S(2)}, u32[]{:S(2)}) %collective-permute-start.38) | collective-permute-done | bytes 524320 | tf_op jit(solution)/shard_map/ppermute | solution.py:35
  392.5 13.8 %collective-permute-done.40 = bf16[256,2048]{1,0:T(8,128)(2,1)} collective-permute-done((bf16[256,2048]{1,0:T(8,128)(2,1)}, bf16[256,2048]{1,0:T(8,128)(2,1)}, u32[]{:S(2)}, u32[]{:S(2)}) %collective-permute-start.40) | collective-permute-done | bytes 1048608 | tf_op jit(solution)/shard_map/ppermute | solution.py:31
  418.8 19.6 %shard_map.215 = (bf16[1024,1536]{1,0:T(8,128)(2,1)}, f32[1,1536]{1,0:T(1,128)S(1)}) custom-call(bf16[4,256,1536]{2,1,0:T(8,128)(2,1)} %get-tuple-element.131.qkv_ref, bf16[1024,512]{1,0:T(8,128)(2,1)S(1)} %shard_map.214.slope_ref, f32[4,256,128]{2,1,0:T(8,128)S(1)} %copy-done.18, f32[4,256,128]{2,1,0:T(8,128)S(1)} %copy-done.16, ...), custom_call_target="tpu_custom_call" | custom-call | tf_op jit(solution)/shard_map/pallas_call | solution.py:554
  476.4 6.7 %shard_map.219 = f32[512,2048]{1,0:T(8,128)S(1)} custom-call(bf16[1024,1536]{1,0:T(8,128)(2,1)S(1)} %copy-done.3, bf16[2048,2048]{1,0:T(8,128)(2,1)} %all-gather.4.cloned.1.call-done.right_ref), custom_call_target="tpu_custom_call" | custom-call | tf_op jit(solution)/shard_map/pallas_call | solution.py:488
  483.1 12.5 %collective-permute-done.49 = bf16[128,2816]{1,0:T(8,128)(2,1)} collective-permute-done((bf16[128,2816]{1,0:T(8,128)(2,1)}, bf16[128,2816]{1,0:T(8,128)(2,1)}, u32[]{:S(2)}, u32[]{:S(2)}) %collective-permute-start.49) | collective-permute-done | bytes 720928 | tf_op jit(solution)/shard_map/ppermute | solution.py:164
  498.8 8.0 %collective-permute-start.54 = (bf16[128,2048]{1,0:T(8,128)(2,1)S(1)}, bf16[128,2048]{1,0:T(8,128)(2,1)S(1)}, u32[]{:S(2)}, u32[]{:S(2)}) collective-permute-start(bf16[128,2048]{1,0:T(8,128)(2,1)S(1)} %slice.490), channel_id=1, source_target_pairs={{0,2},{2,0},{1,3},{3,1},{4,6},{6,4},{5,7},{7,5},{8,10},{10,8},{9,1... | collective-permute-start | bytes 1572872 | tf_op jit(solution)/shard_map/ppermute | solution.py:35
  544.7 6.9 %collective-permute-done.63 = f32[14336]{0:T(1024)S(1)} collective-permute-done((f32[14336]{0:T(1024)S(1)}, f32[14336]{0:T(1024)S(1)}, u32[]{:S(2)}, u32[]{:S(2)}) %collective-permute-start.63) | collective-permute-done | bytes 57376 | tf_op jit(solution)/shard_map/ppermute | solution.py:597
  582.1 7.0 %collective-permute-start.67 = (bf16[128,512]{1,0:T(8,128)(2,1)S(1)}, bf16[128,512]{1,0:T(8,128)(2,1)S(1)}, u32[]{:S(2)}, u32[]{:S(2)}) collective-permute-start(bf16[128,512]{1,0:T(8,128)(2,1)S(1)} %get-tuple-element.317), channel_id=1, source_target_pairs={{2,0},{0,1},{3,2},{1,3},{6,4},{4,5},{7,6},{5,7},{10,8},{8,9},{11,1... | collective-permute-start | bytes 393224 | tf_op jit(solution)/shard_map/ppermute | solution.py:164
  (506 shorter events, 315.3 us)
Async XLA Ops:
  7.2 108.4 %all-gather.4.cloned.1.call-start = ((), (), s32[]{:S(2)}) async-start(), calls=%async_computation.4 | async-start | bytes 9437184 | tf_op jit(solution)/shard_map/all_gather | solution.py:127
  27.4 201.0 %all-gather.6.cloned.1.call-start = ((), (), s32[]{:S(2)}) async-start(), calls=%async_computation.5 | async-start | bytes 12976128 | tf_op jit(solution)/shard_map/all_gather | solution.py:127
  43.9 40.5 %collective-permute-start.9 = (bf16[256,2048]{1,0:T(8,128)(2,1)S(1)}, bf16[256,2048]{1,0:T(8,128)(2,1)S(1)}, u32[]{:S(2)}, u32[]{:S(2)}) collective-permute-start(bf16[256,2048]{1,0:T(8,128)(2,1)S(1)} %pad_maximum_fusion.5), channel_id=1, source_target_pairs={{0,16},{16,0},{1,17},{17,1},{2,18},{18,2},{3,19},{19,3},{4,20},{20... | collective-permute-start | bytes 3145736 | tf_op jit(solution)/shard_map/ppermute | solution.py:31
  45.6 39.8 %collective-permute-start.8 = (bf16[256,2048]{1,0:T(8,128)(2,1)S(1)}, bf16[256,2048]{1,0:T(8,128)(2,1)}, u32[]{:S(2)}, u32[]{:S(2)}) collective-permute-start(bf16[256,2048]{1,0:T(8,128)(2,1)S(1)} %pad_maximum_fusion.4), channel_id=1, source_target_pairs={{0,2},{2,0},{1,3},{3,1},{4,6},{6,4},{5,7},{7,5},{8,10},{10,8},{9,1... | collective-permute-start | bytes 3145736 | tf_op jit(solution)/shard_map/ppermute | solution.py:35
  48.2 36.2 %collective-permute-start.11 = (bf16[128,2816]{1,0:T(8,128)(2,1)S(1)}, bf16[128,2816]{1,0:T(8,128)(2,1)S(1)}, u32[]{:S(2)}, u32[]{:S(2)}) collective-permute-start(bf16[128,2816]{1,0:T(8,128)(2,1)S(1)} %pad_maximum_fusion.14), channel_id=1, source_target_pairs={{0,2},{1,0},{2,3},{3,1},{4,6},{5,4},{6,7},{7,5},{8,10},{9,8},{10,1... | collective-permute-start | bytes 2162696 | tf_op jit(solution)/shard_map/ppermute | solution.py:114
  86.7 194.8 %all-gather.8.cloned.1.call-start = ((), (), s32[]{:S(2)}) async-start(), calls=%async_computation.6 | async-start | bytes 6488064 | tf_op jit(solution)/shard_map/all_gather | solution.py:127
  97.2 45.9 %collective-permute-start.22 = (bf16[128,1408]{1,0:T(8,128)(2,1)}, bf16[128,1408]{1,0:T(8,128)(2,1)}, u32[]{:S(2)}, u32[]{:S(2)}) collective-permute-start(bf16[128,1408]{1,0:T(8,128)(2,1)} %get-tuple-element.269), channel_id=1, source_target_pairs={{0,2},{1,0},{2,3},{3,1},{4,6},{5,4},{6,7},{7,5},{8,10},{9,8},{10,1... | collective-permute-start | bytes 1081352 | tf_op jit(solution)/shard_map/ppermute | solution.py:114
  99.8 44.4 %collective-permute-start.21 = (bf16[128,1408]{1,0:T(8,128)(2,1)}, bf16[128,1408]{1,0:T(8,128)(2,1)}, u32[]{:S(2)}, u32[]{:S(2)}) collective-permute-start(bf16[128,1408]{1,0:T(8,128)(2,1)} %get-tuple-element.145), channel_id=1, source_target_pairs={{1,2},{2,1},{5,6},{6,5},{9,10},{10,9},{13,14},{14,13},{17,18},{18,... | collective-permute-start | bytes 1081352 | tf_op jit(solution)/shard_map/ppermute | solution.py:113
  102.5 41.7 %collective-permute-start.20 = (bf16[128,2048]{1,0:T(8,128)(2,1)}, bf16[128,2048]{1,0:T(8,128)(2,1)}, u32[]{:S(2)}, u32[]{:S(2)}) collective-permute-start(bf16[128,2048]{1,0:T(8,128)(2,1)} %get-tuple-element.291), channel_id=1, source_target_pairs={{0,2},{2,0},{1,3},{3,1},{4,6},{6,4},{5,7},{7,5},{8,10},{10,8},{9,1... | collective-permute-start | bytes 1572872 | tf_op jit(solution)/shard_map/ppermute | solution.py:35
  103.5 40.6 %collective-permute-start.19 = (bf16[128,2048]{1,0:T(8,128)(2,1)}, bf16[128,2048]{1,0:T(8,128)(2,1)}, u32[]{:S(2)}, u32[]{:S(2)}) collective-permute-start(bf16[128,2048]{1,0:T(8,128)(2,1)} %get-tuple-element.292), channel_id=1, source_target_pairs={{0,16},{16,0},{1,17},{17,1},{2,18},{18,2},{3,19},{19,3},{4,20},{20... | collective-permute-start | bytes 1572872 | tf_op jit(solution)/shard_map/ppermute | solution.py:31
  173.0 171.1 %reduce-scatter.5.cloned.1.call-start = ((), (), s32[]{:S(2)}) async-start(), calls=%async_computation.7 | async-start | bytes 3604480 | tf_op jit(solution)/shard_map/reduce_scatter | solution.py:131
  273.3 183.9 %reduce-scatter.7.cloned.1.call-start = ((), (), s32[]{:S(2)}) async-start(), calls=%async_computation.8 | async-start | bytes 7208960 | tf_op jit(solution)/shard_map/reduce_scatter | solution.py:131
  344.2 219.2 %reduce-scatter.9.cloned.1.call-start = ((), (), s32[]{:S(2)}) async-start(), calls=%async_computation.9 | async-start | bytes 3932160 | tf_op jit(solution)/shard_map/reduce_scatter | solution.py:131
  410.6 27.7 %collective-permute-start.42 = (bf16[256,2048]{1,0:T(8,128)(2,1)}, bf16[256,2048]{1,0:T(8,128)(2,1)}, u32[]{:S(2)}, u32[]{:S(2)}) collective-permute-start(bf16[256,2048]{1,0:T(8,128)(2,1)} %get-tuple-element.251), channel_id=1, source_target_pairs={{0,16},{16,0},{1,17},{17,1},{2,18},{18,2},{3,19},{19,3},{4,20},{20... | collective-permute-start | bytes 3145736 | tf_op jit(solution)/shard_map/ppermute | solution.py:31
  412.3 26.1 %collective-permute-start.41 = (bf16[256,2048]{1,0:T(8,128)(2,1)}, bf16[256,2048]{1,0:T(8,128)(2,1)}, u32[]{:S(2)}, u32[]{:S(2)}) collective-permute-start(bf16[256,2048]{1,0:T(8,128)(2,1)} %get-tuple-element.252), channel_id=1, source_target_pairs={{0,2},{2,0},{1,3},{3,1},{4,6},{6,4},{5,7},{7,5},{8,10},{10,8},{9,1... | collective-permute-start | bytes 3145736 | tf_op jit(solution)/shard_map/ppermute | solution.py:35
  449.2 33.9 %collective-permute-start.50 = (bf16[256,1408]{1,0:T(8,128)(2,1)}, bf16[256,1408]{1,0:T(8,128)(2,1)}, u32[]{:S(2)}, u32[]{:S(2)}) collective-permute-start(bf16[256,1408]{1,0:T(8,128)(2,1)} %pad_maximum_fusion.16), channel_id=1, source_target_pairs={{0,16},{16,0},{1,17},{17,1},{2,18},{18,2},{3,19},{19,3},{4,20},{20... | collective-permute-start | bytes 2162696 | tf_op jit(solution)/shard_map/ppermute | solution.py:31
  460.4 35.2 %collective-permute-start.47 = (bf16[256,2048]{1,0:T(8,128)(2,1)}, bf16[256,2048]{1,0:T(8,128)(2,1)}, u32[]{:S(2)}, u32[]{:S(2)}) collective-permute-start(bf16[256,2048]{1,0:T(8,128)(2,1)} %get-tuple-element.249), channel_id=1, source_target_pairs={{0,16},{16,0},{1,17},{17,1},{2,18},{18,2},{3,19},{19,3},{4,20},{20... | collective-permute-start | bytes 3145736 | tf_op jit(solution)/shard_map/ppermute | solution.py:31
  462.1 33.6 %collective-permute-start.46 = (bf16[256,2048]{1,0:T(8,128)(2,1)}, bf16[256,2048]{1,0:T(8,128)(2,1)}, u32[]{:S(2)}, u32[]{:S(2)}) collective-permute-start(bf16[256,2048]{1,0:T(8,128)(2,1)} %get-tuple-element.250), channel_id=1, source_target_pairs={{0,2},{2,0},{1,3},{3,1},{4,6},{6,4},{5,7},{7,5},{8,10},{10,8},{9,1... | collective-permute-start | bytes 3145736 | tf_op jit(solution)/shard_map/ppermute | solution.py:35
  465.6 30.0 %collective-permute-start.49 = (bf16[128,2816]{1,0:T(8,128)(2,1)}, bf16[128,2816]{1,0:T(8,128)(2,1)}, u32[]{:S(2)}, u32[]{:S(2)}) collective-permute-start(bf16[128,2816]{1,0:T(8,128)(2,1)} %get-tuple-element.267), channel_id=1, source_target_pairs={{2,0},{0,1},{3,2},{1,3},{6,4},{4,5},{7,6},{5,7},{10,8},{8,9},{11,1... | collective-permute-start | bytes 2162696 | tf_op jit(solution)/shard_map/ppermute | solution.py:164
  465.6 30.0 %collective-permute-start.48 = (bf16[128,2816]{1,0:T(8,128)(2,1)}, bf16[128,2816]{1,0:T(8,128)(2,1)}, u32[]{:S(2)}, u32[]{:S(2)}) collective-permute-start(bf16[128,2816]{1,0:T(8,128)(2,1)} %get-tuple-element.195), channel_id=1, source_target_pairs={{2,1},{1,2},{6,5},{5,6},{10,9},{9,10},{14,13},{13,14},{18,17},{17,... | collective-permute-start | bytes 2162696 | tf_op jit(solution)/shard_map/ppermute | solution.py:163
  475.9 101.1 %reduce-scatter.11.cloned.1.call-start = ((), (), s32[]{:S(2)}) async-start(), calls=%async_computation.10 | async-start | bytes 1310720 | tf_op jit(solution)/shard_map/reduce_scatter | solution.py:131
  498.4 26.4 %collective-permute-start.53 = (bf16[128,2048]{1,0:T(8,128)(2,1)S(1)}, bf16[128,2048]{1,0:T(8,128)(2,1)S(1)}, u32[]{:S(2)}, u32[]{:S(2)}) collective-permute-start(bf16[128,2048]{1,0:T(8,128)(2,1)S(1)} %slice.491), channel_id=1, source_target_pairs={{0,16},{16,0},{1,17},{17,1},{2,18},{18,2},{3,19},{19,3},{4,20},{20... | collective-permute-start | bytes 1572872 | tf_op jit(solution)/shard_map/ppermute | solution.py:31
  498.8 26.4 %collective-permute-start.54 = (bf16[128,2048]{1,0:T(8,128)(2,1)S(1)}, bf16[128,2048]{1,0:T(8,128)(2,1)S(1)}, u32[]{:S(2)}, u32[]{:S(2)}) collective-permute-start(bf16[128,2048]{1,0:T(8,128)(2,1)S(1)} %slice.490), channel_id=1, source_target_pairs={{0,2},{2,0},{1,3},{3,1},{4,6},{6,4},{5,7},{7,5},{8,10},{10,8},{9,1... | collective-permute-start | bytes 1572872 | tf_op jit(solution)/shard_map/ppermute | solution.py:35
  524.8 38.5 %collective-permute-start.56 = (bf16[256,2816]{1,0:T(8,128)(2,1)}, bf16[256,2816]{1,0:T(8,128)(2,1)}, u32[]{:S(2)}, u32[]{:S(2)}) collective-permute-start(bf16[256,2816]{1,0:T(8,128)(2,1)} %pad_maximum_fusion.3), channel_id=1, source_target_pairs={{0,16},{16,0},{1,17},{17,1},{2,18},{18,2},{3,19},{19,3},{4,20},{20... | collective-permute-start | bytes 4325384 | tf_op jit(solution)/shard_map/ppermute | solution.py:31
  (136 other events, 1273.3 us)
Sparse Core Ops, SparseCore 0:
  27.6 84.8 all-gather.3
  114.1 106.3 all-gather.5
  222.8 58.7 all-gather.7
  283.7 54.8 reduce-scatter.4
  344.3 99.4 reduce-scatter.6
  476.0 58.9 reduce-scatter.8
  540.1 27.1 reduce-scatter.10
